TPU v7x, 512 devices: a whole 4x4x16 slice. The times are simulated.
512 devices in a mesh: fft: 16 (over z_lo, core), band: 32 (over z_hi, y, x).
Axes of the slice: x: 4, y: 4, z: 16 (z_hi: 2, z_lo: 8; z = z_hi * 8 + z_lo), core: 2. Of those that a mesh axis runs over, the one named last changes fastest.
Arguments:
- orbitals: float32 [2, 32, 3584, 128], P(None, 'band', 'fft'), may hold values from -6 to 6
- potential: float32 [128, 128, 128], P('fft'), may hold values from -6 to 6
- stick_coords: int32 [2, 3584], replicated, may hold values from -32 to 32, as said below
- stick_half: int32 [3584], replicated, may hold values from -1 to 32, as said below
Outputs:
- applied: float32 [2, 32, 3584, 128], P(None, 'band', 'fft')
- subspace: float32 [2, 2, 32, 32], replicated
Inputs may be any that keep to these rules, and one draw needn't show every extreme that they name: `stick_coords`: the slots with stick_half >= 0 are exactly the columns (gx, gy) with gx**2 + gy**2 <= 32**2, each once, in an order drawn from the seed; the other slots have arbitrary coordinates in range. For a real stick, stick_half is the largest h with gx**2 + gy**2 + h**2 <= 32**2; empty slots hold -1.
All inputs are finite; a program needn't handle non-finite values.
Results may differ from a plain program's by a relative error of at most 0.0003.
Values may be sent and summed in bfloat16 or wider, within the bound.
No kernel may reach another device: no remote copies, remote signals or barrier semaphores. Data moves between devices by JAX's collectives and lax.ppermute only.
A program may use at most 128 MiB of HBM per device.

v0:
```python
from functools import partial
import math

import jax
import jax.numpy as jnp
from jax import lax
from jax.sharding import PartitionSpec as P

RADIUS = 32
WINDOW = 128


def phase_table(first_set, second_set, grid_len):
    product = first_set[:, None] * second_set[None, :] % grid_len
    angle = product.astype(jnp.float32) * (2.0 * math.pi / grid_len)
    return (jnp.cos(angle), jnp.sin(angle))


def transform(couple, cosine, sine, orient, formula):
    contract = partial(jnp.einsum, formula, precision=lax.Precision.HIGHEST)
    real_part = couple[0]
    imag_part = couple[1]
    new_real = contract(real_part, cosine) - orient * contract(imag_part, sine)
    new_imag = orient * contract(real_part, sine) + contract(imag_part, cosine)
    return jnp.stack([new_real, new_imag])


def correlation_pair(first_set, second_set, factor):
    formula = "bsk,csk->bc"
    dotted = partial(jnp.einsum, formula, preferred_element_type=jnp.float32)
    real_sum = dotted(first_set[0], second_set[0]) + dotted(first_set[1], second_set[1])
    imag_sum = dotted(first_set[0], second_set[1]) - dotted(first_set[1], second_set[0])
    return jnp.stack([real_sum, imag_sum]) * factor


def local(orbitals, potential, stick_coords, stick_half):
    band_dev = orbitals.shape[1]
    stick_dev = orbitals.shape[2]
    slots = orbitals.shape[3]
    planes = potential.shape[0]
    grid_len = potential.shape[1]
    all_sticks = stick_half.shape[0]
    first = lax.axis_index("fft") * stick_dev
    own_coords = lax.dynamic_slice_in_dim(stick_coords, first, stick_dev, 1)
    own_half = lax.dynamic_slice_in_dim(stick_half, first, stick_dev, 0)
    offsets = jnp.arange(slots, dtype=jnp.int32) - RADIUS
    validity = (jnp.abs(offsets)[None, :] <= own_half[:, None]).astype(jnp.float32)
    squares = own_coords[0][:, None] ** 2 + own_coords[1][:, None] ** 2 + offsets[None, :] ** 2
    kinetic = squares.astype(jnp.float32) / (RADIUS * RADIUS)
    coeffs = orbitals * validity
    positions = jnp.arange(grid_len, dtype=jnp.int32)
    z_cos, z_sin = phase_table(offsets, positions, grid_len)
    window_offsets = jnp.arange(WINDOW, dtype=jnp.int32) - RADIUS
    w_cos, w_sin = phase_table(window_offsets, positions, grid_len)
    flat_index = (stick_coords[0] + RADIUS) * WINDOW + (stick_coords[1] + RADIUS)
    cells = WINDOW * WINDOW
    real_cells = jnp.where(stick_half >= 0, flat_index, cells)
    cell_owner = (
        jnp.full((cells,), all_sticks, jnp.int32)
        .at[real_cells]
        .set(jnp.arange(all_sticks, dtype=jnp.int32), mode="drop")
    )
    along_z = transform(coeffs, z_cos, z_sin, 1.0, "bsk,kz->bzs")
    inverse_volume = 1.0 / grid_len**3
    received = lax.all_to_all(along_z, "fft", split_axis=2, concat_axis=3, tiled=True)
    count = received.shape[1]
    field = jnp.take(received, cell_owner, axis=3, mode="fill", fill_value=0.0)
    field = field.reshape(2, count, planes, WINDOW, WINDOW)
    field = transform(field, w_cos, w_sin, 1.0, "bpuv,vy->bpuy")
    field = transform(field, w_cos, w_sin, 1.0, "bpuy,ux->bpxy")
    field = field * potential[None, None]
    field = transform(field, w_cos, w_sin, -1.0, "bpxy,ux->bpuy")
    field = transform(field, w_cos, w_sin, -1.0, "bpuy,vy->bpuv")
    picked = field.reshape(2, count, planes, cells)[:, :, :, flat_index] * inverse_volume
    mixed = lax.all_to_all(picked, "fft", split_axis=3, concat_axis=2, tiled=True)
    potential_part = transform(mixed, z_cos, z_sin, -1.0, "bzs,kz->bsk")
    applied = (kinetic * coeffs + potential_part) * validity
    left = coeffs.astype(jnp.bfloat16)
    right = applied.astype(jnp.bfloat16)
    factor = 1.0 / RADIUS**3
    total_bands = band_dev * lax.axis_size("band")
    initial = jnp.zeros((2, 2, total_bands, band_dev), jnp.float32)
    piece = lax.all_gather(left, "band", axis=1, tiled=True)
    block = jnp.stack(
        [correlation_pair(piece, right, factor), correlation_pair(piece, left, factor)]
    )
    partial_block = lax.dynamic_update_slice_in_dim(initial, block, jnp.int32(0), 2)
    summed = lax.psum(partial_block, "fft")
    subspace = lax.all_gather(summed, "band", axis=3, tiled=True)
    return (applied, subspace)


def solution(mesh):
    return jax.shard_map(
        local,
        mesh=mesh,
        in_specs=(P(None, "band", "fft", None), P("fft", None, None), P(), P()),
        out_specs=(P(None, "band", "fft", None), P()),
        check_vma=False,
    )
```

profile of v0, /device:TPU:0, one launch (start us, length us, event | category | flops | bytes accessed | tf_op | source)
XLA Modules:
  0.0 562.6 jit_solution(4556350407120797541)
XLA Ops:
  8.1 1.6 fusion.244
  12.9 7.2 %all-to-all-start = ((f32[2,1,128,224]{3,1,0,2:T(1,128)}), f32[2,1,128,224]{3,1,0,2:T(1,128)S(1)}, u32[]{:S(2)}, u32[]{:S(2)}) async-start(f32[2,1,128,224]{3,1,0,2:T(1,128)} %copy.24), calls=%async_computation | async-start | bytes 524288 | tf_op jit(solution)/shard_map/all_to_all | solution.py:65
  21.1 13.7 %scatter_custom_fusion = s32[16384]{0:T(1024)S(1)} fusion(s32[3584]{0:T(1024)S(1)} %compare_select_fusion.2, s32[3584]{0:T(1024)S(1)} %iota.68, s32[]{:T(128)} %constant.28.clone.1), kind=kCustom, calls=%fused_computation.130 | custom fusion | bytes 65540 | tf_op jit(solution)/shard_map/scatter | solution.py:61
  35.2 3.5 copy.50
  38.8 113.3 %gather_fusion = f32[16384,2,8]{2,1,0:T(2,128)} fusion(f32[2,8,3584]{1,0,2:T(2,128)} %bitcast.200, s32[16384]{0:T(1024)S(1)} %fusion.113), kind=kCustom, calls=%fused_computation | custom fusion | bytes 2162688 | tf_op jit(solution)/shard_map/jit(_take)/gather | solution.py:67
  152.1 59.0 %bitcast_select_fusion = f32[2,1,8,16384]{2,0,3,1:T(2,128)} fusion(f32[16384,2,8]{2,1,0:T(2,128)} %gather_fusion, pred[16384]{0:T(1024)(128)(4,1)S(1)} %compare_and_fusion), kind=kLoop, calls=%fused_computation.3 | loop fusion | flops 262144 | bytes 2113536 | tf_op jit(solution)/shard_map/jit(_take)/select_n | solution.py:67
  211.1 19.2 %fusion.245 = (f32[1,1,8,16384]{2,0,3,1:T(1,128)}, f32[1,1,8,16384]{2,0,3,1:T(1,128)}) fusion(f32[2,1,8,16384]{2,0,3,1:T(2,128)} %bitcast_select_fusion), kind=kLoop, calls=%fused_computation.244 | loop fusion | bytes 2097152 | tf_op jit(solution)/shard_map/slice | solution.py:22
  230.3 5.1 copy.51
  236.3 0.9 fusion.108
  237.2 5.6 copy.52
  242.8 0.9 convolution_subtract_fusion.1
  243.7 0.9 fusion.100
  244.6 0.9 fusion.89
  246.4 0.9 fusion.5
  247.4 0.9 fusion.4
  250.2 0.9 fusion.3
  252.0 0.9 fusion.1
  252.9 0.9 fusion
  253.8 0.9 convolution_multiply_fusion
  254.7 0.9 convolution_add_fusion
  255.8 14.7 %copy.34 = f32[2,1,8,16384]{2,0,3,1:T(2,128)} copy(f32[2,1,8,16384]{3,2,1,0:T(8,128)S(1)} %pad_maximum_fusion) | data formatting | bytes 2097152 | tf_op jit(solution)/shard_map/stack | solution.py:25
  270.5 17.7 %gather_fusion.1 = f32[3584,2,8]{2,1,0:T(2,128)} fusion(f32[2,8,16384]{1,0,2:T(2,128)} %bitcast.198, s32[4096]{0:T(1024)S(1)} %pad_clamp_fusion), kind=kCustom, calls=%fused_computation.1 | custom fusion | bytes 473088 | tf_op jit(solution)/shard_map/gather | solution.py:74
  288.1 5.1 fusion.246
  293.3 7.3 %reshape.526 = f32[16,1,3584]{2,1,0:T(1,128)} reshape(f32[3584,1,2,8]{3,2,1,0:T(2,128)} %fusion.246) | data formatting | bytes 458752
  300.5 9.7 %all-to-all-start.1 = ((f32[16,1,3584]{2,1,0:T(1,128)}), f32[16,1,3584]{2,1,0:T(1,128)S(1)}, u32[]{:S(2)}, u32[]{:S(2)}) async-start(f32[16,1,3584]{2,1,0:T(1,128)} %reshape.526), calls=%async_computation.1 | async-start | bytes 458752 | tf_op jit(solution)/shard_map/all_to_all | solution.py:75
  310.5 14.0 %all-to-all-done.1 = f32[16,1,3584]{2,1,0:T(1,128)S(1)} async-done(((f32[16,1,3584]{2,1,0:T(1,128)}), f32[16,1,3584]{2,1,0:T(1,128)S(1)}, u32[]{:S(2)}, u32[]{:S(2)}) %all-to-all-start.1) | async-done | bytes 229408 | tf_op jit(solution)/shard_map/all_to_all | solution.py:75
  325.0 1.2 reduce.3
  326.2 7.4 %reshape.527 = f32[3584,1,2,8]{3,2,1,0:T(2,128)} reshape(f32[16,3584]{1,0:T(8,128)S(1)} %reduce.3) | data formatting | bytes 458752
  333.6 4.3 copy.36
  340.9 2.3 slice_bitcast_fusion
  348.3 50.2 %psum.7 = f32[2,2,32,1]{2,3,1,0:T(1,128)S(1)} all-reduce(f32[2,2,32,1]{2,3,1,0:T(1,128)S(1)} %pad_maximum_fusion.2), channel_id=1, replica_groups=mesh['fft'=16,'band'=32] {'fft'}, use_global_device_ids=true, to_apply=%region_1.2 | all-reduce | flops 128 | bytes 1024 | tf_op jit(solution)/shard_map/psum | solution.py:88
  398.5 156.3 %all_gather.7 = f32[2,2,32,32]{2,1,0,3:T(2,128)S(1)} all-gather(f32[2,2,32,1]{2,1,0,3:T(2,128)S(1)} %bitcast.206), channel_id=1, replica_groups=mesh['fft'=16,'band'=32] {'band'}, dimensions={3}, use_global_device_ids=true | all-gather | bytes 16896 | tf_op jit(solution)/shard_map/all_gather | solution.py:89
  (61 shorter events, 19.6 us)
Async XLA Ops:
  8.0 12.9 %copy-start.2 = (s32[2,3584]{1,0:T(2,128)S(1)}, s32[2,3584]{1,0:T(2,128)}, u32[]{:S(2)}) copy-start(s32[2,3584]{1,0:T(2,128)} %param.6) | copy-start | bytes 86020
  8.1 12.9 %copy-start.3 = (s32[3584]{0:T(1024)S(1)}, s32[3584]{0:T(1024)}, u32[]{:S(2)}) copy-start(s32[3584]{0:T(1024)} %param.7) | copy-start | bytes 43012
  12.9 22.3 %all-to-all-start = ((f32[2,1,128,224]{3,1,0,2:T(1,128)}), f32[2,1,128,224]{3,1,0,2:T(1,128)S(1)}, u32[]{:S(2)}, u32[]{:S(2)}) async-start(f32[2,1,128,224]{3,1,0,2:T(1,128)} %copy.24), calls=%async_computation | async-start | bytes 524288 | tf_op jit(solution)/shard_map/all_to_all | solution.py:65
  20.1 320.8 %all-gather.2.cloned.1.call-start = ((), (), s32[]{:S(2)}) async-start(), calls=%async_computation.2 | async-start | bytes 3784704 | tf_op jit(solution)/shard_map/all_gather | solution.py:83
  246.4 1.9 copy-start.1
  293.3 17.2 %copy-start = (bf16[2,1,224,128]{3,2,1,0:T(8,128)(2,1)S(1)}, bf16[2,1,224,128]{3,2,1,0:T(8,128)(2,1)}, u32[]{:S(2)}) copy-start(bf16[2,1,224,128]{3,2,1,0:T(8,128)(2,1)} %get-tuple-element.10) | copy-start | bytes 344068
  300.5 24.0 %all-to-all-start.1 = ((f32[16,1,3584]{2,1,0:T(1,128)}), f32[16,1,3584]{2,1,0:T(1,128)S(1)}, u32[]{:S(2)}, u32[]{:S(2)}) async-start(f32[16,1,3584]{2,1,0:T(1,128)} %reshape.526), calls=%async_computation.1 | async-start | bytes 458752 | tf_op jit(solution)/shard_map/all_to_all | solution.py:75
Sparse Core Ops, SparseCore 0:
  25.4 157.4 all-gather.1
where the time goes:
time: 569 us; the launch traced here: 563 us
  local copies, waits for them, and re-layouts  217 us (38%)
  blocking collectives  207 us (36%)
  other arithmetic  68.4 us (12%)
  matrix products  23.7 us (4%)
  starting transfers between devices  17 us (3%)
  waiting for transfers between devices  15.1 us (3%)
  between operations  14.7 us (3%)
    all_gather x1, blocking collectives, local(): subspace = lax.all_gather(summed, 'band', axis=3, tiled=True)  156 us
    gather x1, local copies, waits for them, and re-layouts, local(): field = jnp.take(received, cell_owner, axis=3, mode='fill', fill_value=0.0)  113 us
    select_n x1, other arithmetic, local(): field = jnp.take(received, cell_owner, axis=3, mode='fill', fill_value=0.0)  59 us
    psum x1, blocking collectives, local(): summed = lax.psum(partial_block, 'fft')  50.2 us
    slice x1, local copies, waits for them, and re-layouts, transform(): imag_part = couple[1]  19.2 us
    gather x1, local copies, waits for them, and re-layouts, local(): field.reshape(2, count, planes, cells)[:, :, :, flat_index] * inverse_volume  17.7 us
    another operation x4, local copies, waits for them, and re-layouts, transform(): return jnp.stack([new_real, new_imag])  15.7 us
    unnamed x11, local copies, waits for them, and re-layouts  15.4 us
  transfers between devices with their start and end apart: 3, of which 2 were waited for; matrix products, arithmetic and copies ran while one was open for 53% of the time, Pallas kernels for 0%

commit v1 on v0

v1 whole, which is shorter than its diff:
```python
import math

import jax
import jax.numpy as jnp
import ml_dtypes
import numpy as np
from jax import lax
from jax.experimental import pallas as pl
from jax.experimental.pallas import tpu as pltpu
from jax.sharding import Mesh
from jax.sharding import PartitionSpec as P

RADIUS = 32
GRID = 128
SLOTS = 128
FFT = 16
OWN = 224
PAD = 256
PLANES = 8
GROUPS = 17
ROWS = GROUPS * 2 * PLANES
KX = 144
F32 = jnp.float32
BF16 = jnp.bfloat16
FULL = ("zlo", "core", "zhi", "y", "x")
VMEM = 48 * 1024 * 1024


def halves(table):
    high = table.astype(ml_dtypes.bfloat16)
    low = (table - high.astype(np.float64)).astype(ml_dtypes.bfloat16)
    return high, low


def waves(first, second):
    angle = (np.outer(first, second) % GRID) * (2.0 * math.pi / GRID)
    return np.cos(angle), np.sin(angle)


def z_table():
    cos, sin = waves(np.arange(GRID), np.arange(SLOTS) - RADIUS)
    cos[:, 2 * RADIUS + 1 :] = 0.0
    sin[:, 2 * RADIUS + 1 :] = 0.0
    real = np.concatenate([cos, -sin], axis=1).reshape(FFT, 1, PLANES, 2 * SLOTS)
    imag = np.concatenate([sin, cos], axis=1).reshape(FFT, 1, PLANES, 2 * SLOTS)
    return np.concatenate([real, imag], axis=1).reshape(2 * GRID, 2 * SLOTS)


def y_table():
    cos, sin = waves(np.arange(64) - RADIUS, np.arange(GRID))
    return np.tile(np.concatenate([cos, sin], axis=1), (4, 1))


def x_table():
    v = 4 * np.arange(GROUPS)[None, :] + np.arange(4)[:, None]
    freq = np.where(v <= 2 * RADIUS, v - RADIUS, 0).reshape(-1)
    cos, sin = waves(np.arange(GRID), freq)
    table = np.zeros((2 * GRID, KX))
    table[:GRID, :68], table[:GRID, 68:136] = cos, -sin
    table[GRID:, :68], table[GRID:, 68:136] = sin, cos
    return table


def y_back_table():
    cos, sin = waves(np.arange(GRID), np.arange(64) - RADIUS)
    real = np.concatenate([cos, sin], axis=0)
    imag = np.concatenate([-sin, cos], axis=0)
    return np.stack([np.tile(real, (1, 4)), np.tile(imag, (1, 4))]) * (1.0 / GRID**3)


def split(value):
    high = value.astype(BF16)
    return high, (value - high.astype(F32)).astype(BF16)


def dot(left, right):
    return jnp.dot(left, right, preferred_element_type=F32)


def dot3(left, right):
    return dot(left[0], right[0]) + dot(left[1], right[0]) + dot(left[0], right[1])


def masked(orbitals, rows):
    cols = jnp.transpose(rows)[:OWN]
    offset = lax.broadcasted_iota(jnp.int32, (OWN, SLOTS), 1).astype(F32) - RADIUS
    valid = jnp.abs(offset) <= cols[:, 0:1]
    real = jnp.where(valid, orbitals[0, 0], 0.0)
    imag = jnp.where(valid, orbitals[1, 0], 0.0)
    kinetic = (cols[:, 1:2] + offset * offset) * (1.0 / (RADIUS * RADIUS))
    return real, imag, valid, kinetic


def pack(real, imag):
    lane = lax.broadcasted_iota(jnp.int32, real.shape, 1)
    first = lane < 64
    main = jnp.where(first, real, pltpu.roll(imag, 64, 1))
    last = jnp.where(first, pltpu.roll(real, 64, 1), imag)
    last = jnp.where(lane % 64 == 0, last, 0.0)
    return main + jnp.concatenate([last[OWN - 1 :], last[: OWN - 1]], axis=0)


def z_kernel(orb_ref, rows_ref, high_ref, low_ref, out_ref, left_ref):
    real, imag, _, _ = masked(orb_ref, rows_ref[...])
    both = jnp.concatenate([real, imag], axis=1)
    both = jnp.concatenate([both, jnp.zeros((PAD - OWN, 2 * SLOTS), F32)], axis=0)
    high, low = split(both)
    contract = (((1,), (1,)), ((), ()))

    def product(a, b):
        return lax.dot_general(a, b, contract, preferred_element_type=F32)

    out = product(high_ref[...], high) + product(high_ref[...], low) + product(low_ref[...], high)
    out_ref[...] = out.reshape(FFT, 2 * PLANES, PAD)
    left_ref[...] = pack(real, imag).astype(BF16)


def plane_kernel(
    val_ref,
    group_ref,
    col_ref,
    colt_ref,
    pot_ref,
    yh_ref,
    yl_ref,
    xh_ref,
    xl_ref,
    bxh_ref,
    bxl_ref,
    byh_ref,
    byl_ref,
    out_ref,
    spread_ref,
    hot_ref,
    t_ref,
    g_ref,
):
    block = 2 * PLANES
    for c in range(FFT):
        value = val_ref[c]
        high = value.astype(BF16).astype(F32)
        low = value - high
        group = group_ref[c : c + 1, :]
        for r in range(GROUPS):
            here = jnp.broadcast_to(group == r, (block, PAD))
            spread_ref[r * block : (r + 1) * block, c * PAD : (c + 1) * PAD] = jnp.where(here, high, 0.0).astype(BF16)
            spread_ref[ROWS + r * block : ROWS + (r + 1) * block, c * PAD : (c + 1) * PAD] = jnp.where(here, low, 0.0).astype(BF16)
        lane = lax.broadcasted_iota(jnp.int32, (PAD, 256), 1)
        hot_ref[c * PAD : (c + 1) * PAD, :] = jnp.where(lane == colt_ref[:, c : c + 1], 1.0, 0.0).astype(BF16)
    window = dot(spread_ref[...], hot_ref[...])
    window = window[:ROWS] + window[ROWS:]

    quarter = lax.broadcasted_iota(jnp.int32, (ROWS, 256), 1) // 64
    stacked = jnp.concatenate([jnp.where(quarter == q, window, 0.0) for q in range(4)], axis=0)
    along = dot3(split(stacked), (yh_ref[...], yl_ref[...]))
    along = along.reshape(4, GROUPS, 2, PLANES, 256)
    real = along[:, :, 0, :, :GRID] - along[:, :, 1, :, GRID:]
    imag = along[:, :, 0, :, GRID:] + along[:, :, 1, :, :GRID]
    parity = lax.broadcasted_iota(jnp.int32, (PLANES, GRID), 1) % 2
    sign = jnp.where(parity == 1, -1.0, 1.0)
    half = 4 * GROUPS * PLANES
    t_ref[:half, :] = real.reshape(half, GRID)
    t_ref[half:, :] = imag.reshape(half, GRID)
    special = (GROUPS + 16) * PLANES
    for base in (special, half + special):
        t_ref[base : base + PLANES, :] = t_ref[base : base + PLANES, :] * sign

    count = 2 * 4 * GROUPS
    fill = jnp.zeros((KX - count, 256), F32)
    for pair in range(PLANES // 2):
        p = 2 * pair
        planes = [t_ref[pl.ds(p + i, count, stride=PLANES), :] for i in range(2)]
        part = jnp.concatenate([jnp.concatenate(planes, axis=1), fill], axis=0)
        field = dot3((xh_ref[...], xl_ref[...]), split(part))
        pot = jnp.concatenate([pot_ref[p], pot_ref[p + 1]], axis=1)
        field = field * jnp.concatenate([pot, pot], axis=0)
        back = dot3((bxh_ref[...], bxl_ref[...]), split(field))
        for i in range(2):
            g_ref[pl.ds(p + i, count, stride=PLANES), :] = back[:count, i * GRID : (i + 1) * GRID]
    for base in (special, half + special):
        g_ref[base : base + PLANES, :] = g_ref[base : base + PLANES, :] * sign

    couple = split(jnp.concatenate([g_ref[:half, :], g_ref[half:, :]], axis=1))
    parts = []
    rows = GROUPS * PLANES
    quarter = lax.broadcasted_iota(jnp.int32, (rows, 256), 1) // 64
    for i in range(2):
        cells = dot3(couple, (byh_ref[i], byl_ref[i]))
        total = jnp.zeros((rows, 256), F32)
        for q in range(4):
            total = jnp.where(quarter == q, cells[q * rows : (q + 1) * rows], total)
        parts.append(total.reshape(GROUPS, 1, PLANES, 256))
    cells = jnp.concatenate(parts, axis=1).reshape(ROWS, 256)
    high, low = split(cells)
    cells = jnp.concatenate([high, low], axis=0)

    sub = lax.broadcasted_iota(jnp.int32, (256, PAD), 0)
    for c in range(FFT):
        hot = jnp.where(sub == col_ref[c : c + 1, :], 1.0, 0.0).astype(BF16)
        found = dot(cells, hot)
        found = found[:ROWS] + found[ROWS:]
        group = group_ref[c : c + 1, :]
        total = jnp.zeros((block, PAD), F32)
        for r in range(GROUPS):
            here = jnp.broadcast_to(group == r, (block, PAD))
            total = jnp.where(here, found[r * block : (r + 1) * block], total)
        out_ref[c] = total


def apply_kernel(mix_ref, orb_ref, rows_ref, high_ref, low_ref, applied_ref, right_ref):
    real, imag, valid, kinetic = masked(orb_ref, rows_ref[...])
    mixed = dot3((high_ref[...], low_ref[...]), split(mix_ref[...].reshape(256, PAD)))
    mixed_real = jnp.transpose(mixed[:SLOTS])[:OWN]
    mixed_imag = jnp.transpose(mixed[SLOTS:])[:OWN]
    applied_real = jnp.where(valid, kinetic * real + mixed_real, 0.0)
    applied_imag = jnp.where(valid, kinetic * imag + mixed_imag, 0.0)
    applied_ref[0, 0] = applied_real
    applied_ref[1, 0] = applied_imag
    right_ref[...] = pack(applied_real, applied_imag).astype(BF16)


def column_kernel(all_ref, left_ref, right_ref, side_ref, out_ref, sums_ref, second_ref):
    groups, sides = all_ref.shape[0], all_ref.shape[1]
    bands = groups * sides
    lane = lax.broadcasted_iota(jnp.int32, (OWN, SLOTS), 1)
    sign = jnp.where(lane < 64, 1.0, -1.0)
    right = right_ref[...].astype(F32)
    left = left_ref[...].astype(F32)
    second_ref[0] = right
    second_ref[1] = pltpu.roll(right, 64, 1) * sign
    second_ref[2] = left
    second_ref[3] = pltpu.roll(left, 64, 1) * sign
    side = side_ref[0]
    for s in range(sides):
        def one(g, carry, s=s):
            row = ((side + s) % sides) * groups + g
            mine = all_ref[g, s].astype(F32)
            for t in range(4):
                product = (mine * second_ref[t]).reshape(OWN // 8, 8, SLOTS)
                sums_ref[pl.ds((t * bands + row) * 8, 8), :] = jnp.sum(product, axis=0)
            return carry

        lax.fori_loop(0, groups, one, 0)
    total = jnp.sum(sums_ref[...].reshape(4 * bands, 8, SLOTS), axis=1)
    ones = jnp.ones((8, SLOTS), F32)
    summed = lax.dot_general(
        ones, total, (((1,), (1,)), ((), ())), precision=lax.Precision.HIGHEST, preferred_element_type=F32
    )
    out_ref[...] = summed * (1.0 / RADIUS**3)


def call(kernel, out_shape, scratch=(), flops=10**8, smem=None, count=0):
    specs = [pl.BlockSpec(memory_space=pltpu.VMEM)] * count
    if smem is not None:
        specs[smem] = pl.BlockSpec(memory_space=pltpu.SMEM)
    return pl.pallas_call(
        kernel,
        out_shape=out_shape,
        in_specs=specs,
        scratch_shapes=list(scratch),
        compiler_params=pltpu.CompilerParams(vmem_limit_bytes=VMEM),
        cost_estimate=pl.CostEstimate(flops=flops, bytes_accessed=10**6, transcendentals=0),
    )


def solution(mesh):
    fft, band = mesh.shape["fft"], mesh.shape["band"]
    shape = (fft // 2, 2) + ((2, 4, 4) if band == 32 else (1, 1, band))
    fine = Mesh(mesh.devices.reshape(shape), FULL)
    sides, groups = shape[2], shape[3] * shape[4]
    bands = sides * groups
    shaped = jax.ShapeDtypeStruct

    zh, zl = halves(z_table())
    yh, yl = halves(y_table())
    xh, xl = halves(x_table())
    byh, byl = halves(y_back_table())

    def local(orbitals, potential, stick_coords, stick_half):
        me = lax.axis_index(("zlo", "core"))
        gx, gy = stick_coords[0], stick_coords[1]
        rows = jnp.stack([stick_half, gx * gx + gy * gy]).astype(F32)
        rows = lax.dynamic_slice_in_dim(rows, me * OWN, OWN, 1)
        rows = jnp.pad(rows, ((0, 6), (0, PAD - OWN)))

        sent, left = call(
            z_kernel,
            [shaped((FFT, 2 * PLANES, PAD), F32), shaped((OWN, SLOTS), BF16)],
            count=4,
        )(orbitals, rows, zh, zl)
        received = lax.all_to_all(sent, ("zlo", "core"), 0, 0, tiled=True)

        edge = gy == RADIUS
        v = jnp.where(edge, 2 * RADIUS + 1, gx + RADIUS)
        u = jnp.where(edge, 0, gy + RADIUS)
        group = jnp.where(stick_half >= 0, v // 4, -1)
        col = (v % 4) * 64 + u
        group = jnp.pad(group.reshape(FFT, OWN), ((0, 0), (0, PAD - OWN)), constant_values=-1)
        col = jnp.pad(col.reshape(FFT, OWN), ((0, 0), (0, PAD - OWN)))

        other = lax.ppermute(left, "zhi", [(i, (i + 1) % sides) for i in range(sides)]) if sides > 1 else None
        both = jnp.stack([left, other]) if sides > 1 else left[None]
        spread = jnp.broadcast_to(both[None], (groups,) + both.shape)
        everyone = lax.all_to_all(spread, ("y", "x"), 0, 0, tiled=True)

        picked = call(
            plane_kernel,
            shaped((FFT, 2 * PLANES, PAD), F32),
            scratch=[
                pltpu.VMEM((2 * ROWS, FFT * PAD), BF16),
                pltpu.VMEM((FFT * PAD, 256), BF16),
                pltpu.VMEM((2 * 4 * GROUPS * PLANES, GRID), F32),
                pltpu.VMEM((2 * 4 * GROUPS * PLANES, GRID), F32),
            ],
            flops=4 * 10**9,
            count=13,
        )(received, group, col, col.T, potential, yh, yl, xh, xl, xh.T, xl.T, byh, byl)
        mixed = lax.all_to_all(picked, ("zlo", "core"), 0, 0, tiled=True)
        applied, right = call(
            apply_kernel,
            [shaped(orbitals.shape, F32), shaped((OWN, SLOTS), BF16)],
            count=5,
        )(mixed, orbitals, rows, zh.T, zl.T)

        side = lax.axis_index("zhi").astype(jnp.int32).reshape(1)
        column = call(
            column_kernel,
            shaped((8, 4 * bands), F32),
            scratch=[pltpu.VMEM((4 * bands * 8, SLOTS), F32), pltpu.VMEM((4, OWN, SLOTS), F32)],
            smem=3,
            count=4,
        )(everyone, left, right, side)
        column = jnp.broadcast_to(column[:1][None], (fft * sides, 1, 4 * bands))
        column = lax.all_to_all(column, ("zlo", "core", "zhi"), 0, 0, tiled=True)
        column = jnp.sum(column.reshape(fft, sides, 4 * bands), axis=0)
        column = jnp.broadcast_to(column[None], (groups, sides, 4 * bands))
        columns = lax.all_to_all(column, ("y", "x"), 0, 0, tiled=True)
        columns = columns.reshape(groups, sides, 4, bands)
        subspace = jnp.transpose(columns, (2, 3, 1, 0)).reshape(2, 2, bands, bands)
        return applied, subspace

    across = ("zhi", "y", "x")
    along = ("zlo", "core")
    return jax.shard_map(
        local,
        mesh=fine,
        in_specs=(P(None, across, along, None), P(along, None, None), P(), P()),
        out_specs=(P(None, across, along, None), P()),
        check_vma=False,
    )
```

time: 569 us -> 143 us (0.25)
  the two profiles are of different devices: /device:TPU:0 before, /device:TPU:1 now
where the time goes in v1:
time: 143 us; the launch traced here: 142 us
  waiting for transfers between devices  50.6 us (35%)
  blocking collectives  35.5 us (25%)
  starting transfers between devices  34.2 us (24%)
  Pallas kernels  12.4 us (9%)
  local copies, waits for them, and re-layouts  6.58 us (5%)
  other arithmetic  1.84 us (1%)
    all_to_all x1, blocking collectives, local(): column = lax.all_to_all(column, ('zlo', 'core', 'zhi'), 0, 0, tiled=True)  26.5 us
    all_to_all x1, waiting for transfers between devices, local(): everyone = lax.all_to_all(spread, ('y', 'x'), 0, 0, tiled=True)  22.5 us
    all_to_all x1, waiting for transfers between devices, local(): received = lax.all_to_all(sent, ('zlo', 'core'), 0, 0, tiled=True)  15.7 us
    all_to_all x1, starting transfers between devices, local(): received = lax.all_to_all(sent, ('zlo', 'core'), 0, 0, tiled=True)  14 us
    all_to_all x1, blocking collectives, local(): columns = lax.all_to_all(column, ('y', 'x'), 0, 0, tiled=True)  8.98 us
    pallas_call x1, Pallas kernels, local(): call(plane_kernel, shaped((FFT, 2 * PLANES, PAD), F32), scratch=[pltpu.VM...  8.22 us
    ppermute x1, starting transfers between devices, local(): lax.ppermute(left, 'zhi', [(i, (i + 1) % sides) for i in range(sides)])  7.95 us
    all_to_all x1, starting transfers between devices, local(): everyone = lax.all_to_all(spread, ('y', 'x'), 0, 0, tiled=True)  6.88 us
  transfers between devices with their start and end apart: 4, of which 4 were waited for; matrix products, arithmetic and copies ran while one was open for 1% of the time, Pallas kernels for 1%

profile of v1, /device:TPU:1, one launch (start us, length us, event | category | flops | bytes accessed | tf_op | source)
XLA Modules:
  0.0 141.9 jit_solution(287664445123322321)
XLA Ops:
  0.6 0.0 copy-start.9
  0.6 0.8 stack.16
  1.4 0.9 fusion.7
  2.3 0.1 fusion.9
  2.4 0.9 copy-done
  3.4 0.9 copy-done.4
  4.3 0.9 copy-done.5
  5.3 1.2 shard_map.167
  6.5 14.0 %all-to-all-start = ((f32[16,16,256]{2,1,0:T(8,128)}), f32[16,16,256]{2,1,0:T(8,128)S(1)}, u32[]{:S(2)}, u32[]{:S(2)}) async-start(f32[16,16,256]{2,1,0:T(8,128)} %get-tuple-element.6), calls=%async_computation | async-start | bytes 524288 | tf_op jit(solution)/shard_map/all_to_all | solution.py:291
  20.5 0.1 select_n.46
  20.6 0.1 select_n.43
  20.6 0.7 fusion.4
  21.4 0.1 reshape.43
  21.5 0.1 copy.70
  21.6 0.1 copy.74
  21.7 0.1 fusion.2
  21.7 0.1 copy.83
  21.8 15.7 %all-to-all-done.val_ref = f32[16,16,256]{2,1,0:T(8,128)S(1)} async-done(((f32[16,16,256]{2,1,0:T(8,128)}), f32[16,16,256]{2,1,0:T(8,128)S(1)}, u32[]{:S(2)}, u32[]{:S(2)}) %all-to-all-start) | async-done | bytes 262176 | tf_op jit(solution)/shard_map/all_to_all | solution.py:291
  37.6 8.2 %shard_map.168 = f32[16,16,256]{2,1,0:T(8,128)} custom-call(f32[16,16,256]{2,1,0:T(8,128)S(1)} %all-to-all-done.val_ref, s32[16,256]{1,0:T(8,128)S(1)} %pad.12.group_ref, s32[16,256]{1,0:T(8,128)S(1)} %pad.13.clone.col_ref, s32[256,16]{1,0:T(8,128)S(1)} %pad_bitcast_fusion.colt_ref, f32[8,128,128]{2,1,0:T(8,128)S(1)} %copy-done.6, ...), custom_call_target="tpu_custom_call" | custom-call | flops 4000000000 | bytes 1000000 | tf_op jit(solution)/shard_map/pallas_call | solution.py:306
  45.8 5.3 %all-to-all-start.1 = ((f32[16,16,256]{2,1,0:T(8,128)}), f32[16,16,256]{2,1,0:T(8,128)S(1)}, u32[]{:S(2)}, u32[]{:S(2)}) async-start(f32[16,16,256]{2,1,0:T(8,128)} %shard_map.168), calls=%async_computation.1 | async-start | bytes 524288 | tf_op jit(solution)/shard_map/all_to_all | solution.py:318
  51.1 7.9 %collective-permute-start = (bf16[224,128]{1,0:T(8,128)(2,1)S(1)}, bf16[224,128]{1,0:T(8,128)(2,1)S(1)}, u32[]{:S(2)}, u32[]{:S(2)}) collective-permute-start(bf16[224,128]{1,0:T(8,128)(2,1)S(1)} %get-tuple-element.8.left_ref), channel_id=1, source_target_pairs={{0,16},{16,0},{1,17},{17,1},{2,18},{18,2},{3,19},{19,3},{4,20},{20... | collective-permute-start | bytes 172040 | tf_op jit(solution)/shard_map/ppermute | solution.py:301
  59.0 6.1 %collective-permute-done = bf16[224,128]{1,0:T(8,128)(2,1)S(1)} collective-permute-done((bf16[224,128]{1,0:T(8,128)(2,1)S(1)}, bf16[224,128]{1,0:T(8,128)(2,1)S(1)}, u32[]{:S(2)}, u32[]{:S(2)}) %collective-permute-start) | collective-permute-done | bytes 57376 | tf_op jit(solution)/shard_map/ppermute | solution.py:301
  65.2 6.3 %all-to-all-done.1.mix_ref = f32[16,16,256]{2,1,0:T(8,128)S(1)} async-done(((f32[16,16,256]{2,1,0:T(8,128)}), f32[16,16,256]{2,1,0:T(8,128)S(1)}, u32[]{:S(2)}, u32[]{:S(2)}) %all-to-all-start.1) | async-done | bytes 262176 | tf_op jit(solution)/shard_map/all_to_all | solution.py:318
  71.4 1.6 %broadcast_in_dim.28 = bf16[16,2,224,128]{3,2,1,0:T(8,128)(2,1)} broadcast(bf16[2,224,128]{2,1,0:T(8,128)(2,1)S(1)} %pad_maximum_fusion), dimensions={1,2,3} | broadcast | bytes 1949696 | tf_op jit(solution)/shard_map/broadcast_in_dim | solution.py:303
  73.1 6.9 %all-to-all-start.2 = ((bf16[16,2,224,128]{3,2,1,0:T(8,128)(2,1)}), bf16[16,2,224,128]{3,2,1,0:T(8,128)(2,1)S(1)}, u32[]{:S(2)}, u32[]{:S(2)}) async-start(bf16[16,2,224,128]{3,2,1,0:T(8,128)(2,1)} %broadcast_in_dim.28), calls=%async_computation.2 | async-start | bytes 3670016 | tf_op jit(solution)/shard_map/all_to_all | solution.py:304
  80.0 1.1 shard_map.169
  81.1 22.5 %all-to-all-done.2.all_ref = bf16[16,2,224,128]{3,2,1,0:T(8,128)(2,1)S(1)} async-done(((bf16[16,2,224,128]{3,2,1,0:T(8,128)(2,1)}), bf16[16,2,224,128]{3,2,1,0:T(8,128)(2,1)S(1)}, u32[]{:S(2)}, u32[]{:S(2)}) %all-to-all-start.2) | async-done | bytes 1835040 | tf_op jit(solution)/shard_map/all_to_all | solution.py:304
  103.6 1.9 %shard_map.170 = f32[8,128]{1,0:T(8,128)S(1)} custom-call(bf16[16,2,224,128]{3,2,1,0:T(8,128)(2,1)S(1)} %all-to-all-done.2.all_ref, bf16[224,128]{1,0:T(8,128)(2,1)S(1)} %get-tuple-element.8.left_ref, bf16[224,128]{1,0:T(8,128)(2,1)S(1)} %get-tuple-element.9.right_ref, s32[1]{0:T(128)} %bitcast.3.side_ref), custom_call_target="tpu_custom_call" | custom-call | flops 100000000 | bytes 1000000 | tf_op jit(solution)/shard_map/pallas_call | solution.py:326
  105.5 26.5 %all_to_all.25 = f32[32,1,128]{2,1,0:T(1,128)S(1)} all-to-all(f32[32,1,128]{2,1,0:T(1,128)S(1)} %broadcast_in_dim.30), channel_id=1, replica_groups=mesh['zlo'=8,'core'=2,'zhi'=2,'y'=4,'x'=4] {'zlo','core','zhi'}, dimensions={0} | all-to-all | bytes 32768 | tf_op jit(solution)/shard_map/all_to_all | solution.py:334
  132.1 9.0 %all_to_all.26 = f32[16,2,128]{2,1,0:T(2,128)S(1)} all-to-all(f32[16,2,128]{2,1,0:T(2,128)S(1)} %broadcast_in_dim.31), channel_id=1, replica_groups=mesh['zlo'=8,'core'=2,'zhi'=2,'y'=4,'x'=4] {'y','x'}, dimensions={0} | all-to-all | bytes 32768 | tf_op jit(solution)/shard_map/all_to_all | solution.py:337
  141.1 0.1 reshape.46
  141.2 0.7 copy.79
  (36 shorter events, 0.2 us)
Async XLA Ops:
  0.6 36.9 %copy-start.9 = (bf16[256,144]{1,0:T(8,128)(2,1)S(1)}, bf16[256,144]{1,0:T(8,128)(2,1)}, u32[]{:S(2)}) copy-start(bf16[256,144]{1,0:T(8,128)(2,1)} %constant.90.clone.xl_ref) | copy-start | bytes 221188
  2.4 0.9 copy-start
  3.4 0.9 copy-start.4
  4.3 0.9 copy-start.5
  5.2 32.3 %copy-start.6 = (f32[8,128,128]{2,1,0:T(8,128)S(1)}, f32[8,128,128]{2,1,0:T(8,128)}, u32[]{:S(2)}) copy-start(f32[8,128,128]{2,1,0:T(8,128)} %pot_ref.1) | copy-start | bytes 1572868
  5.2 32.3 %copy-start.7 = (bf16[2,256,256]{2,1,0:T(8,128)(2,1)S(1)}, bf16[2,256,256]{2,1,0:T(8,128)(2,1)}, u32[]{:S(2)}) copy-start(bf16[2,256,256]{2,1,0:T(8,128)(2,1)} %constant.94.clone.byl_ref) | copy-start | bytes 786436
  5.2 32.3 %copy-start.8 = (bf16[2,256,256]{2,1,0:T(8,128)(2,1)S(1)}, bf16[2,256,256]{2,1,0:T(8,128)(2,1)}, u32[]{:S(2)}) copy-start(bf16[2,256,256]{2,1,0:T(8,128)(2,1)} %constant.93.clone.byh_ref) | copy-start | bytes 786436
  5.2 32.3 %copy-start.10 = (bf16[256,144]{1,0:T(8,128)(2,1)S(1)}, bf16[256,144]{1,0:T(8,128)(2,1)}, u32[]{:S(2)}) copy-start(bf16[256,144]{1,0:T(8,128)(2,1)} %constant.89.clone.xh_ref) | copy-start | bytes 221188
  5.2 32.3 %copy-start.11 = (bf16[256,256]{1,0:T(8,128)(2,1)S(1)}, bf16[256,256]{1,0:T(8,128)(2,1)}, u32[]{:S(2)}) copy-start(bf16[256,256]{1,0:T(8,128)(2,1)} %constant.88.clone.yl_ref) | copy-start | bytes 393220
  5.2 32.3 %copy-start.12 = (bf16[256,256]{1,0:T(8,128)(2,1)S(1)}, bf16[256,256]{1,0:T(8,128)(2,1)}, u32[]{:S(2)}) copy-start(bf16[256,256]{1,0:T(8,128)(2,1)} %constant.87.clone.yh_ref) | copy-start | bytes 393220
  5.2 32.3 %copy-start.13 = (bf16[144,256]{1,0:T(8,128)(2,1)S(1)}, bf16[144,256]{1,0:T(8,128)(2,1)}, u32[]{:S(2)}) copy-start(bf16[144,256]{1,0:T(8,128)(2,1)} %constant.92.clone.bxl_ref) | copy-start | bytes 221188
  5.2 32.3 %copy-start.14 = (bf16[144,256]{1,0:T(8,128)(2,1)S(1)}, bf16[144,256]{1,0:T(8,128)(2,1)}, u32[]{:S(2)}) copy-start(bf16[144,256]{1,0:T(8,128)(2,1)} %constant.91.clone.bxh_ref) | copy-start | bytes 221188
  6.5 31.0 %all-to-all-start = ((f32[16,16,256]{2,1,0:T(8,128)}), f32[16,16,256]{2,1,0:T(8,128)S(1)}, u32[]{:S(2)}, u32[]{:S(2)}) async-start(f32[16,16,256]{2,1,0:T(8,128)} %get-tuple-element.6), calls=%async_computation | async-start | bytes 524288 | tf_op jit(solution)/shard_map/all_to_all | solution.py:291
  45.8 25.7 %all-to-all-start.1 = ((f32[16,16,256]{2,1,0:T(8,128)}), f32[16,16,256]{2,1,0:T(8,128)S(1)}, u32[]{:S(2)}, u32[]{:S(2)}) async-start(f32[16,16,256]{2,1,0:T(8,128)} %shard_map.168), calls=%async_computation.1 | async-start | bytes 524288 | tf_op jit(solution)/shard_map/all_to_all | solution.py:318
  51.1 14.1 %collective-permute-start = (bf16[224,128]{1,0:T(8,128)(2,1)S(1)}, bf16[224,128]{1,0:T(8,128)(2,1)S(1)}, u32[]{:S(2)}, u32[]{:S(2)}) collective-permute-start(bf16[224,128]{1,0:T(8,128)(2,1)S(1)} %get-tuple-element.8.left_ref), channel_id=1, source_target_pairs={{0,16},{16,0},{1,17},{17,1},{2,18},{18,2},{3,19},{19,3},{4,20},{20... | collective-permute-start | bytes 172040 | tf_op jit(solution)/shard_map/ppermute | solution.py:301
  73.1 6.9 %copy-start.1 = (f32[2,1,224,128]{3,2,1,0:T(8,128)S(1)}, f32[2,1,224,128]{3,2,1,0:T(8,128)}, u32[]{:S(2)}) copy-start(f32[2,1,224,128]{3,2,1,0:T(8,128)} %orb_ref.3) | copy-start | bytes 688132
  73.1 6.9 %copy-start.2 = (bf16[256,256]{1,0:T(8,128)(2,1)S(1)}, bf16[256,256]{1,0:T(8,128)(2,1)}, u32[]{:S(2)}) copy-start(bf16[256,256]{1,0:T(8,128)(2,1)} %constant.96.clone.low_ref) | copy-start | bytes 393220
  73.1 6.9 %copy-start.3 = (bf16[256,256]{1,0:T(8,128)(2,1)S(1)}, bf16[256,256]{1,0:T(8,128)(2,1)}, u32[]{:S(2)}) copy-start(bf16[256,256]{1,0:T(8,128)(2,1)} %constant.95.clone.high_ref) | copy-start | bytes 393220
  73.1 30.5 %all-to-all-start.2 = ((bf16[16,2,224,128]{3,2,1,0:T(8,128)(2,1)}), bf16[16,2,224,128]{3,2,1,0:T(8,128)(2,1)S(1)}, u32[]{:S(2)}, u32[]{:S(2)}) async-start(bf16[16,2,224,128]{3,2,1,0:T(8,128)(2,1)} %broadcast_in_dim.28), calls=%async_computation.2 | async-start | bytes 3670016 | tf_op jit(solution)/shard_map/all_to_all | solution.py:304

commit v2 on v1

--- a/solution.py
+++ b/solution.py
@@ -16,6 +16,7 @@
 FFT = 16
 OWN = 224
 PAD = 256
+LEVELS = 32767.0
 PLANES = 8
 GROUPS = 17
 ROWS = GROUPS * 2 * PLANES
@@ -81,8 +82,24 @@
     return dot(left[0], right[0]) + dot(left[1], right[0]) + dot(left[0], right[1])
 
 
-def masked(orbitals, rows):
-    cols = jnp.transpose(rows)[:OWN]
+def encode(value):
+    top = jnp.max(jnp.max(jnp.abs(value), axis=1, keepdims=True), axis=2, keepdims=True)
+    power = jnp.floor(jnp.log2(jnp.maximum(top, 1e-30))) + 1.0
+    size = jnp.maximum(jnp.abs(value) * jnp.exp2(-power), 1e-30)
+    size = jnp.minimum(jnp.exp2(jnp.log2(size) * (1.0 / 3.0)) * LEVELS + 0.5, LEVELS)
+    size = jnp.floor(size)
+    coded = jnp.where(value < 0.0, -size, size)
+    lane = lax.broadcasted_iota(jnp.int32, value.shape, 2)
+    return jnp.where(lane == OWN, power, coded).astype(jnp.int32).astype(jnp.int16)
+
+
+def decode(coded):
+    coded = coded.astype(jnp.int32).astype(F32)
+    return coded * coded * coded * (jnp.exp2(coded[:, :, OWN : OWN + 1]) * (1.0 / LEVELS**3))
+
+
+def masked(orbitals, cols):
+    cols = cols[:OWN]
     offset = lax.broadcasted_iota(jnp.int32, (OWN, SLOTS), 1).astype(F32) - RADIUS
     valid = jnp.abs(offset) <= cols[:, 0:1]
     real = jnp.where(valid, orbitals[0, 0], 0.0)
@@ -100,19 +117,39 @@
     return main + jnp.concatenate([last[OWN - 1 :], last[: OWN - 1]], axis=0)
 
 
-def z_kernel(orb_ref, rows_ref, high_ref, low_ref, out_ref, left_ref):
-    real, imag, _, _ = masked(orb_ref, rows_ref[...])
+def z_kernel(orb_hbm, high_hbm, low_hbm, coords_hbm, half_hbm, out_ref, left_ref, cols_ref, orb, high, low, coords, half, sems):
+    pairs = ((half_hbm, half), (coords_hbm, coords), (orb_hbm, orb), (high_hbm, high), (low_hbm, low))
+    copies = [pltpu.make_async_copy(a, b, sems.at[i]) for i, (a, b) in enumerate(pairs)]
+    for copy in copies:
+        copy.start()
+    me = lax.axis_index("zlo") * 2 + lax.axis_index("core")
+    tile = jnp.minimum(me * OWN // 128, 25)
+    shift = me * OWN - tile * 128
+    copies[0].wait()
+    copies[1].wait()
+    wide = pl.ds(pl.multiple_of(tile * 128, 128), 384)
+    own = jnp.concatenate([half[pl.ds(tile + i, 1), :] for i in range(3)], axis=1)
+    own = jnp.concatenate([own, coords[:, wide], jnp.zeros((5, 384), jnp.int32)], axis=0).astype(F32)
+    own = pltpu.roll(own, lax.rem(384 - shift, 384), 1)[:, :PAD]
+    squares = own[1:2] * own[1:2] + own[2:3] * own[2:3]
+    cols = jnp.transpose(jnp.concatenate([own[:1], squares, own[2:]], axis=0))
+    cols_ref[...] = cols
+    copies[2].wait()
+    real, imag, _, _ = masked(orb, cols)
+    left = pack(real, imag).astype(BF16)
+    left_ref[...] = left
     both = jnp.concatenate([real, imag], axis=1)
-    both = jnp.concatenate([both, jnp.zeros((PAD - OWN, 2 * SLOTS), F32)], axis=0)
-    high, low = split(both)
+    both = split(jnp.concatenate([both, jnp.zeros((PAD - OWN, 2 * SLOTS), F32)], axis=0))
     contract = (((1,), (1,)), ((), ()))
 
     def product(a, b):
         return lax.dot_general(a, b, contract, preferred_element_type=F32)
 
-    out = product(high_ref[...], high) + product(high_ref[...], low) + product(low_ref[...], high)
-    out_ref[...] = out.reshape(FFT, 2 * PLANES, PAD)
-    left_ref[...] = pack(real, imag).astype(BF16)
+    copies[3].wait()
+    out = product(high[...], both[0]) + product(high[...], both[1])
+    copies[4].wait()
+    out = out + product(low[...], both[0])
+    out_ref[...] = encode(out.reshape(FFT, 2 * PLANES, PAD))
 
 
 def plane_kernel(
@@ -136,8 +173,9 @@
     g_ref,
 ):
     block = 2 * PLANES
+    values = decode(val_ref[...])
     for c in range(FFT):
-        value = val_ref[c]
+        value = values[c]
         high = value.astype(BF16).astype(F32)
         low = value - high
         group = group_ref[c : c + 1, :]
@@ -204,44 +242,54 @@
         for r in range(GROUPS):
             here = jnp.broadcast_to(group == r, (block, PAD))
             total = jnp.where(here, found[r * block : (r + 1) * block], total)
-        out_ref[c] = total
-
-
-def apply_kernel(mix_ref, orb_ref, rows_ref, high_ref, low_ref, applied_ref, right_ref):
-    real, imag, valid, kinetic = masked(orb_ref, rows_ref[...])
-    mixed = dot3((high_ref[...], low_ref[...]), split(mix_ref[...].reshape(256, PAD)))
+        out_ref[c : c + 1] = encode(total[None])
+
+
+def apply_kernel(mix_ref, orb_ref, cols_ref, high_ref, low_ref, applied_ref, spread_ref):
+    real, imag, valid, kinetic = masked(orb_ref, cols_ref[...])
+    mixed = dot3((high_ref[...], low_ref[...]), split(decode(mix_ref[...]).reshape(256, PAD)))
     mixed_real = jnp.transpose(mixed[:SLOTS])[:OWN]
     mixed_imag = jnp.transpose(mixed[SLOTS:])[:OWN]
     applied_real = jnp.where(valid, kinetic * real + mixed_real, 0.0)
     applied_imag = jnp.where(valid, kinetic * imag + mixed_imag, 0.0)
     applied_ref[0, 0] = applied_real
     applied_ref[1, 0] = applied_imag
-    right_ref[...] = pack(applied_real, applied_imag).astype(BF16)
-
-
-def column_kernel(all_ref, left_ref, right_ref, side_ref, out_ref, sums_ref, second_ref):
-    groups, sides = all_ref.shape[0], all_ref.shape[1]
-    bands = groups * sides
+    right = pack(applied_real, applied_imag).astype(BF16)
+    left = pack(real, imag).astype(BF16)
+    for i in range(spread_ref.shape[0]):
+        spread_ref[i, 0] = right
+        spread_ref[i, 1] = left
+
+
+def block_kernel(left_ref, pair_ref, out_ref, sums_ref, second_ref):
+    depth, sides = left_ref.shape[0], left_ref.shape[1]
+    width = pair_ref.shape[0]
     lane = lax.broadcasted_iota(jnp.int32, (OWN, SLOTS), 1)
     sign = jnp.where(lane < 64, 1.0, -1.0)
-    right = right_ref[...].astype(F32)
-    left = left_ref[...].astype(F32)
-    second_ref[0] = right
-    second_ref[1] = pltpu.roll(right, 64, 1) * sign
-    second_ref[2] = left
-    second_ref[3] = pltpu.roll(left, 64, 1) * sign
-    side = side_ref[0]
-    for s in range(sides):
-        def one(g, carry, s=s):
-            row = ((side + s) % sides) * groups + g
-            mine = all_ref[g, s].astype(F32)
+    side, y = lax.axis_index("zhi"), lax.axis_index("y")
+
+    def column(x, carry):
+        for m in range(2):
+            second = pair_ref[x, m].astype(F32)
+            second_ref[2 * m] = second
+            second_ref[2 * m + 1] = pltpu.roll(second, 64, 1) * sign
+
+        def one(j, carry):
+            order, other = j // sides, lax.rem(j, sides)
+            mine = left_ref[order, other].astype(F32)
+            flip = lax.rem(order, 2)
+            near = y + flip * (1 - 2 * lax.rem(y, 2))
+            row = jnp.where(order >= 2, depth - 1 - near, near) + depth * lax.rem(side + other, sides)
             for t in range(4):
                 product = (mine * second_ref[t]).reshape(OWN // 8, 8, SLOTS)
-                sums_ref[pl.ds((t * bands + row) * 8, 8), :] = jnp.sum(product, axis=0)
+                place = (t * sides * depth + row) * width + x
+                sums_ref[pl.ds(pl.multiple_of(place * 8, 8), 8), :] = jnp.sum(product, axis=0)
             return carry
 
-        lax.fori_loop(0, groups, one, 0)
-    total = jnp.sum(sums_ref[...].reshape(4 * bands, 8, SLOTS), axis=1)
+        return lax.fori_loop(0, depth * sides, one, carry)
+
+    lax.fori_loop(0, width, column, 0)
+    total = jnp.sum(sums_ref[...].reshape(-1, 8, SLOTS), axis=1)
     ones = jnp.ones((8, SLOTS), F32)
     summed = lax.dot_general(
         ones, total, (((1,), (1,)), ((), ())), precision=lax.Precision.HIGHEST, preferred_element_type=F32
@@ -249,17 +297,14 @@
     out_ref[...] = summed * (1.0 / RADIUS**3)
 
 
-def call(kernel, out_shape, scratch=(), flops=10**8, smem=None, count=0):
-    specs = [pl.BlockSpec(memory_space=pltpu.VMEM)] * count
-    if smem is not None:
-        specs[smem] = pl.BlockSpec(memory_space=pltpu.SMEM)
+def call(kernel, out_shape, count, scratch=(), flops=10**8, traffic=10**6, hbm=False, limit=VMEM):
     return pl.pallas_call(
         kernel,
         out_shape=out_shape,
-        in_specs=specs,
+        in_specs=[pl.BlockSpec(memory_space=pl.ANY if hbm else pltpu.VMEM)] * count,
         scratch_shapes=list(scratch),
-        compiler_params=pltpu.CompilerParams(vmem_limit_bytes=VMEM),
-        cost_estimate=pl.CostEstimate(flops=flops, bytes_accessed=10**6, transcendentals=0),
+        compiler_params=pltpu.CompilerParams(vmem_limit_bytes=limit),
+        cost_estimate=pl.CostEstimate(flops=flops, bytes_accessed=traffic, transcendentals=0),
     )
 
 
@@ -267,7 +312,8 @@
     fft, band = mesh.shape["fft"], mesh.shape["band"]
     shape = (fft // 2, 2) + ((2, 4, 4) if band == 32 else (1, 1, band))
     fine = Mesh(mesh.devices.reshape(shape), FULL)
-    sides, groups = shape[2], shape[3] * shape[4]
+    sides, depth, width = shape[2:]
+    groups = depth * width
     bands = sides * groups
     shaped = jax.ShapeDtypeStruct
 
@@ -277,17 +323,23 @@
     byh, byl = halves(y_back_table())
 
     def local(orbitals, potential, stick_coords, stick_half):
-        me = lax.axis_index(("zlo", "core"))
         gx, gy = stick_coords[0], stick_coords[1]
-        rows = jnp.stack([stick_half, gx * gx + gy * gy]).astype(F32)
-        rows = lax.dynamic_slice_in_dim(rows, me * OWN, OWN, 1)
-        rows = jnp.pad(rows, ((0, 6), (0, PAD - OWN)))
-
-        sent, left = call(
+        stick = (OWN, SLOTS)
+        sent, left, cols = call(
             z_kernel,
-            [shaped((FFT, 2 * PLANES, PAD), F32), shaped((OWN, SLOTS), BF16)],
-            count=4,
-        )(orbitals, rows, zh, zl)
+            [shaped((FFT, 2 * PLANES, PAD), jnp.int16), shaped(stick, BF16), shaped((PAD, 8), F32)],
+            5,
+            scratch=[
+                pltpu.VMEM(orbitals.shape, F32),
+                pltpu.VMEM(zh.shape, BF16),
+                pltpu.VMEM(zl.shape, BF16),
+                pltpu.VMEM(stick_coords.shape, jnp.int32),
+                pltpu.VMEM((28, 128), jnp.int32),
+                pltpu.SemaphoreType.DMA((5,)),
+            ],
+            hbm=True,
+            limit=62 * 1024 * 1024,
+        )(orbitals, zh, zl, stick_coords, stick_half.reshape(28, 128))
         received = lax.all_to_all(sent, ("zlo", "core"), 0, 0, tiled=True)
 
         edge = gy == RADIUS
@@ -298,45 +350,47 @@
         group = jnp.pad(group.reshape(FFT, OWN), ((0, 0), (0, PAD - OWN)), constant_values=-1)
         col = jnp.pad(col.reshape(FFT, OWN), ((0, 0), (0, PAD - OWN)))
 
-        other = lax.ppermute(left, "zhi", [(i, (i + 1) % sides) for i in range(sides)]) if sides > 1 else None
-        both = jnp.stack([left, other]) if sides > 1 else left[None]
-        spread = jnp.broadcast_to(both[None], (groups,) + both.shape)
-        everyone = lax.all_to_all(spread, ("y", "x"), 0, 0, tiled=True)
-
         picked = call(
             plane_kernel,
-            shaped((FFT, 2 * PLANES, PAD), F32),
+            shaped((FFT, 2 * PLANES, PAD), jnp.int16),
+            13,
             scratch=[
                 pltpu.VMEM((2 * ROWS, FFT * PAD), BF16),
                 pltpu.VMEM((FFT * PAD, 256), BF16),
                 pltpu.VMEM((2 * 4 * GROUPS * PLANES, GRID), F32),
                 pltpu.VMEM((2 * 4 * GROUPS * PLANES, GRID), F32),
             ],
-            flops=4 * 10**9,
-            count=13,
+            flops=1,
+            traffic=1,
         )(received, group, col, col.T, potential, yh, yl, xh, xl, xh.T, xl.T, byh, byl)
+        lefts = left[None]
+        if sides > 1:
+            far = lax.ppermute(left, "zhi", [(0, 1), (1, 0)])
+            picked, far = lax.optimization_barrier((picked, far))
+            lefts = jnp.stack([left, far])
+        lefts = lefts[None]
+        if depth > 1:
+            lefts = jnp.concatenate([lefts, lax.ppermute(lefts, "y", [(i, i ^ 1) for i in range(depth)])])
+            lefts = jnp.concatenate([lefts, lax.ppermute(lefts, "y", [(i, depth - 1 - i) for i in range(depth)])])
+
         mixed = lax.all_to_all(picked, ("zlo", "core"), 0, 0, tiled=True)
-        applied, right = call(
-            apply_kernel,
-            [shaped(orbitals.shape, F32), shaped((OWN, SLOTS), BF16)],
-            count=5,
-        )(mixed, orbitals, rows, zh.T, zl.T)
-
-        side = lax.axis_index("zhi").astype(jnp.int32).reshape(1)
+        applied, spread = call(apply_kernel, [shaped(orbitals.shape, F32), shaped((width, 2) + stick, BF16)], 5)(
+            mixed, orbitals, cols, zh.T, zl.T
+        )
+        pairs = lax.all_to_all(spread, "x", 0, 0, tiled=True)
         column = call(
-            column_kernel,
+            block_kernel,
             shaped((8, 4 * bands), F32),
-            scratch=[pltpu.VMEM((4 * bands * 8, SLOTS), F32), pltpu.VMEM((4, OWN, SLOTS), F32)],
-            smem=3,
-            count=4,
-        )(everyone, left, right, side)
+            2,
+            scratch=[pltpu.VMEM((4 * bands * 8, SLOTS), F32), pltpu.VMEM((4,) + stick, F32)],
+        )(lefts, pairs)
         column = jnp.broadcast_to(column[:1][None], (fft * sides, 1, 4 * bands))
         column = lax.all_to_all(column, ("zlo", "core", "zhi"), 0, 0, tiled=True)
         column = jnp.sum(column.reshape(fft, sides, 4 * bands), axis=0)
         column = jnp.broadcast_to(column[None], (groups, sides, 4 * bands))
         columns = lax.all_to_all(column, ("y", "x"), 0, 0, tiled=True)
-        columns = columns.reshape(groups, sides, 4, bands)
-        subspace = jnp.transpose(columns, (2, 3, 1, 0)).reshape(2, 2, bands, bands)
+        columns = columns.reshape(depth, width, sides, 4, sides, depth, width)
+        subspace = jnp.transpose(columns, (3, 4, 5, 1, 2, 0, 6)).reshape(2, 2, bands, bands)
         return applied, subspace
 
     across = ("zhi", "y", "x")

time: 143 us -> 107 us (0.75)
  waiting for transfers between devices: 50.6 us -> 14.7 us
  starting transfers between devices: 34.2 us -> 42 us
  blocking collectives: 35.5 us -> 31.5 us
  local copies, waits for them, and re-layouts: 6.58 us -> 2.66 us
  Pallas kernels: 12.4 us -> 14.6 us
  other arithmetic: 1.84 us -> 0.27 us
    all_to_all x1, waiting for transfers between devices: 22.5 us -> 7.56 us  [local(): pairs = lax.all_to_all(spread, 'x', 0, 0, tiled=True)]
    all_to_all x1, waiting for transfers between devices: 15.7 us -> 3.27 us  [local(): received = lax.all_to_all(sent, ('zlo', 'core'), 0, 0, tiled=True)]
    ppermute x1 -> x3, starting transfers between devices: 7.95 us -> 16 us  [the longest x1 7.96 us: local(): far = lax.ppermute(left, 'zhi', [(0, 1), (1, 0)])]
    all_to_all x1, waiting for transfers between devices: 6.27 us -> 0.53 us  [local(): mixed = lax.all_to_all(picked, ('zlo', 'core'), 0, 0, tiled=True)]
    all_to_all x1, blocking collectives: 26.5 us -> 22.4 us  [local(): column = lax.all_to_all(column, ('zlo', 'core', 'zhi'), 0, 0, tiled=True)]
    unnamed x32 -> x33, local copies, waits for them, and re-layouts: 3.59 us -> 0.15 us
    all_to_all x1, starting transfers between devices: 6.88 us -> 4.02 us  [local(): pairs = lax.all_to_all(spread, 'x', 0, 0, tiled=True)]
    ppermute x1 -> x3, waiting for transfers between devices: 6.13 us -> 3.37 us  [the longest x1 3.37 us: local(): lax.ppermute(lefts, 'y', [(i, i ^ 1) for i in range(depth)])]
  transfers between devices with their start and end apart: 4 -> 6, of which waited for: 4 -> 4; matrix products, arithmetic and copies ran while one was open for 1% -> 1% of each run, Pallas kernels for 1% -> 9%
where the time goes in v2:
time: 107 us
  starting transfers between devices  42 us (39%)
  blocking collectives  31.5 us (29%)
  waiting for transfers between devices  14.7 us (14%)
  Pallas kernels  14.6 us (14%)
  local copies, waits for them, and re-layouts  2.66 us (2%)
    all_to_all x1, blocking collectives, local(): column = lax.all_to_all(column, ('zlo', 'core', 'zhi'), 0, 0, tiled=True)  22.4 us
    all_to_all x1, starting transfers between devices, local(): received = lax.all_to_all(sent, ('zlo', 'core'), 0, 0, tiled=True)  14.2 us
    all_to_all x1, blocking collectives, local(): columns = lax.all_to_all(column, ('y', 'x'), 0, 0, tiled=True)  9.09 us
    pallas_call x1, Pallas kernels, local(): call(plane_kernel, shaped((FFT, 2 * PLANES, PAD), jnp.int16), 13, scratch...  8.35 us
    ppermute x1, starting transfers between devices, local(): far = lax.ppermute(left, 'zhi', [(0, 1), (1, 0)])  7.96 us
    all_to_all x1, starting transfers between devices, local(): mixed = lax.all_to_all(picked, ('zlo', 'core'), 0, 0, tiled=True)  7.79 us
    all_to_all x1, waiting for transfers between devices, local(): pairs = lax.all_to_all(spread, 'x', 0, 0, tiled=True)  7.56 us
    ppermute x1, starting transfers between devices, local(): lax.ppermute(lefts, 'y', [(i, depth - 1 - i) for i in range(depth)])  4.64 us
  transfers between devices with their start and end apart: 6, of which 4 were waited for; matrix products, arithmetic and copies ran while one was open for 1% of the time, Pallas kernels for 9%

profile of v2, /device:TPU:1, one launch (start us, length us, event | category | flops | bytes accessed | tf_op | source)
XLA Modules:
  0.0 106.7 jit_solution(16328132785599296204)
XLA Ops:
  0.6 0.0 copy-start.7
  0.7 0.0 copy-start.12
  0.7 2.6 %shard_map.167 = (s16[16,16,256]{2,1,0:T(8,128)(2,1)}, bf16[224,128]{1,0:T(8,128)(2,1)}, f32[256,8]{1,0:T(8,128)}) custom-call(f32[2,1,224,128]{3,2,1,0:T(8,128)} %orb_ref.1, bf16[256,256]{1,0:T(8,128)(2,1)} %constant.63.clone.high_hbm, bf16[256,256]{1,0:T(8,128)(2,1)} %constant.64.clone.low_hbm, s32[2,3584]{1,0:T(2,128)} %coords_hbm.1, s32[28,128]{1,0:T(8,128)} %bitcast.14), custom_call_target="tpu_custom_call" | custom-call | flops 100000000 | bytes 1000000 | tf_op jit(solution)/shard_map/pallas_call | solution.py:328
  3.3 0.0 copy-start.5
  3.3 0.0 copy-start.6
  3.3 14.2 %all-to-all-start = ((s16[16,16,256]{2,1,0:T(8,128)(2,1)}), s16[16,16,256]{2,1,0:T(8,128)(2,1)S(1)}, u32[]{:S(2)}, u32[]{:S(2)}) async-start(s16[16,16,256]{2,1,0:T(8,128)(2,1)} %get-tuple-element.9), calls=%async_computation | async-start | bytes 262144 | tf_op jit(solution)/shard_map/all_to_all | solution.py:343
  17.5 8.0 %collective-permute-start = (bf16[224,128]{1,0:T(8,128)(2,1)}, bf16[224,128]{1,0:T(8,128)(2,1)S(1)}, u32[]{:S(2)}, u32[]{:S(2)}) collective-permute-start(bf16[224,128]{1,0:T(8,128)(2,1)} %get-tuple-element.10), channel_id=1, source_target_pairs={{0,16},{16,0},{1,17},{17,1},{2,18},{18,2},{3,19},{19,3},{4,20},{20... | collective-permute-start | bytes 172040 | tf_op jit(solution)/shard_map/ppermute | solution.py:368
  25.5 0.1 fusion.7
  25.6 0.0 copy-start.4
  25.6 0.1 select_n.42
  25.7 0.1 select_n.39
  25.8 0.1 copy.60
  25.9 0.1 copy.64
  26.0 0.1 fusion.2
  26.1 0.1 copy.70
  26.2 0.1 reshape.43
  26.3 3.3 %all-to-all-done.val_ref = s16[16,16,256]{2,1,0:T(8,128)(2,1)S(1)} async-done(((s16[16,16,256]{2,1,0:T(8,128)(2,1)}), s16[16,16,256]{2,1,0:T(8,128)(2,1)S(1)}, u32[]{:S(2)}, u32[]{:S(2)}) %all-to-all-start) | async-done | bytes 131104 | tf_op jit(solution)/shard_map/all_to_all | solution.py:343
  29.6 8.3 %shard_map.168 = s16[16,16,256]{2,1,0:T(8,128)(2,1)} custom-call(s16[16,16,256]{2,1,0:T(8,128)(2,1)S(1)} %all-to-all-done.val_ref, s32[16,256]{1,0:T(8,128)S(1)} %pad.7.group_ref, s32[16,256]{1,0:T(8,128)S(1)} %pad.8.clone.col_ref, s32[256,16]{1,0:T(8,128)S(1)} %pad_bitcast_fusion.colt_ref, f32[8,128,128]{2,1,0:T(8,128)S(1)} %copy-done.1, ...), custom_call_target="tpu_custom_call" | custom-call | flops 1 | bytes 1 | tf_op jit(solution)/shard_map/pallas_call | solution.py:353
  38.0 7.8 %all-to-all-start.1 = ((s16[16,16,256]{2,1,0:T(8,128)(2,1)}), s16[16,16,256]{2,1,0:T(8,128)(2,1)S(1)}, u32[]{:S(2)}, u32[]{:S(2)}) async-start(s16[16,16,256]{2,1,0:T(8,128)(2,1)} %shard_map.168), calls=%async_computation.1 | async-start | bytes 262144 | tf_op jit(solution)/shard_map/all_to_all | solution.py:376
  45.8 3.4 %collective-permute-start.1 = (bf16[1,2,224,128]{3,2,1,0:T(8,128)(2,1)S(1)}, bf16[1,2,224,128]{3,2,1,0:T(8,128)(2,1)S(1)}, u32[]{:S(2)}, u32[]{:S(2)}) collective-permute-start(bf16[1,2,224,128]{3,2,1,0:T(8,128)(2,1)S(1)} %maximum_bitcast_fusion), channel_id=1, source_target_pairs={{0,4},{4,0},{8,12},{12,8},{1,5},{5,1},{9,13},{13,9},{2,6},{6,2},{1... | collective-permute-start | bytes 344072 | tf_op jit(solution)/shard_map/ppermute | solution.py:373
  49.2 3.4 %collective-permute-done.1 = bf16[1,2,224,128]{3,2,1,0:T(8,128)(2,1)S(1)} collective-permute-done((bf16[1,2,224,128]{3,2,1,0:T(8,128)(2,1)S(1)}, bf16[1,2,224,128]{3,2,1,0:T(8,128)(2,1)S(1)}, u32[]{:S(2)}, u32[]{:S(2)}) %collective-permute-start.1) | collective-permute-done | bytes 114720 | tf_op jit(solution)/shard_map/ppermute | solution.py:373
  52.6 4.6 %collective-permute-start.2 = (bf16[2,2,224,128]{3,2,1,0:T(8,128)(2,1)S(1)}, bf16[2,2,224,128]{3,2,1,0:T(8,128)(2,1)S(1)}, u32[]{:S(2)}, u32[]{:S(2)}) collective-permute-start(bf16[2,2,224,128]{3,2,1,0:T(8,128)(2,1)S(1)} %pad_maximum_fusion.1), channel_id=1, source_target_pairs={{0,12},{4,8},{8,4},{12,0},{1,13},{5,9},{9,5},{13,1},{2,14},{6,10},... | collective-permute-start | bytes 688136 | tf_op jit(solution)/shard_map/ppermute | solution.py:374
  57.3 0.5 all-to-all-done.1.mix_ref
  57.8 1.3 %shard_map.169 = (f32[2,1,224,128]{3,2,1,0:T(8,128)}, bf16[4,2,224,128]{3,2,1,0:T(8,128)(2,1)}) custom-call(s16[16,16,256]{2,1,0:T(8,128)(2,1)S(1)} %all-to-all-done.1.mix_ref, f32[2,1,224,128]{3,2,1,0:T(8,128)S(1)} %copy-done, f32[256,8]{1,0:T(8,128)S(1)} %copy-done.10, bf16[256,256]{1,0:T(8,128)(2,1)S(1)} %copy-done.9, bf16[256,256]{1,0:T(8,128)(2,1)S(1)} %copy-done.8), custom_call_target="tpu_custom_call" | custom-call | flops 100000000 | bytes 1000000 | tf_op jit(solution)/shard_map/pallas_call | solution.py:377
  59.1 4.0 %all-to-all-start.2 = ((bf16[4,2,224,128]{3,2,1,0:T(8,128)(2,1)}), bf16[4,2,224,128]{3,2,1,0:T(8,128)(2,1)S(1)}, u32[]{:S(2)}, u32[]{:S(2)}) async-start(bf16[4,2,224,128]{3,2,1,0:T(8,128)(2,1)} %get-tuple-element.15), calls=%async_computation.2 | async-start | bytes 917504 | tf_op jit(solution)/shard_map/all_to_all | solution.py:380
  63.2 7.6 %all-to-all-done.2.pair_ref = bf16[4,2,224,128]{3,2,1,0:T(8,128)(2,1)S(1)} async-done(((bf16[4,2,224,128]{3,2,1,0:T(8,128)(2,1)}), bf16[4,2,224,128]{3,2,1,0:T(8,128)(2,1)S(1)}, u32[]{:S(2)}, u32[]{:S(2)}) %all-to-all-start.2) | async-done | bytes 458784 | tf_op jit(solution)/shard_map/all_to_all | solution.py:380
  70.7 2.3 %shard_map.170 = f32[8,128]{1,0:T(8,128)S(1)} custom-call(bf16[4,2,224,128]{3,2,1,0:T(8,128)(2,1)S(1)} %pad_maximum_fusion.left_ref, bf16[4,2,224,128]{3,2,1,0:T(8,128)(2,1)S(1)} %all-to-all-done.2.pair_ref), custom_call_target="tpu_custom_call" | custom-call | flops 100000000 | bytes 1000000 | tf_op jit(solution)/shard_map/pallas_call | solution.py:381
  73.1 22.4 %all_to_all.25 = f32[32,1,128]{2,1,0:T(1,128)S(1)} all-to-all(f32[32,1,128]{2,1,0:T(1,128)S(1)} %broadcast_in_dim.27), channel_id=1, replica_groups=mesh['zlo'=8,'core'=2,'zhi'=2,'y'=4,'x'=4] {'zlo','core','zhi'}, dimensions={0} | all-to-all | bytes 32768 | tf_op jit(solution)/shard_map/all_to_all | solution.py:388
  95.6 9.1 %all_to_all.26 = f32[16,2,128]{2,1,0:T(2,128)S(1)} all-to-all(f32[16,2,128]{2,1,0:T(2,128)S(1)} %broadcast_in_dim.28), channel_id=1, replica_groups=mesh['zlo'=8,'core'=2,'zhi'=2,'y'=4,'x'=4] {'y','x'}, dimensions={0} | all-to-all | bytes 32768 | tf_op jit(solution)/shard_map/all_to_all | solution.py:391
  104.6 0.7 reshape.45
  105.3 0.3 copy.68
  105.7 1.0 reshape.46
  (41 shorter events, 0.3 us)
Async XLA Ops:
  0.6 24.9 %copy-start.13 = (s32[2,3584]{1,0:T(2,128)S(1)}, s32[2,3584]{1,0:T(2,128)}, u32[]{:S(2)}) copy-start(s32[2,3584]{1,0:T(2,128)} %coords_hbm.1) | copy-start | bytes 86020
  0.6 25.3 %copy-start.14 = (s32[3584]{0:T(1024)S(1)}, s32[3584]{0:T(1024)}, u32[]{:S(2)}) copy-start(s32[3584]{0:T(1024)} %param.19) | copy-start | bytes 43012
  0.6 28.9 %copy-start.7 = (bf16[256,256]{1,0:T(8,128)(2,1)S(1)}, bf16[256,256]{1,0:T(8,128)(2,1)}, u32[]{:S(2)}) copy-start(bf16[256,256]{1,0:T(8,128)(2,1)} %constant.65.clone.yh_ref) | copy-start | bytes 393220
  0.7 28.9 %copy-start.12 = (bf16[144,256]{1,0:T(8,128)(2,1)S(1)}, bf16[144,256]{1,0:T(8,128)(2,1)}, u32[]{:S(2)}) copy-start(bf16[144,256]{1,0:T(8,128)(2,1)} %constant.69.clone.bxh_ref) | copy-start | bytes 221188
  3.3 26.2 %copy-start.5 = (bf16[256,144]{1,0:T(8,128)(2,1)S(1)}, bf16[256,144]{1,0:T(8,128)(2,1)}, u32[]{:S(2)}) copy-start(bf16[256,144]{1,0:T(8,128)(2,1)} %constant.67.clone.xh_ref) | copy-start | bytes 221188
  3.3 26.2 %copy-start.6 = (bf16[256,256]{1,0:T(8,128)(2,1)S(1)}, bf16[256,256]{1,0:T(8,128)(2,1)}, u32[]{:S(2)}) copy-start(bf16[256,256]{1,0:T(8,128)(2,1)} %constant.66.clone.yl_ref) | copy-start | bytes 393220
  3.3 26.2 %all-to-all-start = ((s16[16,16,256]{2,1,0:T(8,128)(2,1)}), s16[16,16,256]{2,1,0:T(8,128)(2,1)S(1)}, u32[]{:S(2)}, u32[]{:S(2)}) async-start(s16[16,16,256]{2,1,0:T(8,128)(2,1)} %get-tuple-element.9), calls=%async_computation | async-start | bytes 262144 | tf_op jit(solution)/shard_map/all_to_all | solution.py:343
  17.5 20.4 %collective-permute-start = (bf16[224,128]{1,0:T(8,128)(2,1)}, bf16[224,128]{1,0:T(8,128)(2,1)S(1)}, u32[]{:S(2)}, u32[]{:S(2)}) collective-permute-start(bf16[224,128]{1,0:T(8,128)(2,1)} %get-tuple-element.10), channel_id=1, source_target_pairs={{0,16},{16,0},{1,17},{17,1},{2,18},{18,2},{3,19},{19,3},{4,20},{20... | collective-permute-start | bytes 172040 | tf_op jit(solution)/shard_map/ppermute | solution.py:368
  25.5 4.1 %copy-start.11 = (bf16[144,256]{1,0:T(8,128)(2,1)S(1)}, bf16[144,256]{1,0:T(8,128)(2,1)}, u32[]{:S(2)}) copy-start(bf16[144,256]{1,0:T(8,128)(2,1)} %constant.70.clone.bxl_ref) | copy-start | bytes 221188
  25.6 4.0 %copy-start.4 = (bf16[256,144]{1,0:T(8,128)(2,1)S(1)}, bf16[256,144]{1,0:T(8,128)(2,1)}, u32[]{:S(2)}) copy-start(bf16[256,144]{1,0:T(8,128)(2,1)} %constant.68.clone.xl_ref) | copy-start | bytes 221188
  25.8 3.8 %copy-start.3 = (bf16[2,256,256]{2,1,0:T(8,128)(2,1)S(1)}, bf16[2,256,256]{2,1,0:T(8,128)(2,1)}, u32[]{:S(2)}) copy-start(bf16[2,256,256]{2,1,0:T(8,128)(2,1)} %constant.71.clone.byh_ref) | copy-start | bytes 786436
  25.9 3.7 %copy-start.1 = (f32[8,128,128]{2,1,0:T(8,128)S(1)}, f32[8,128,128]{2,1,0:T(8,128)}, u32[]{:S(2)}) copy-start(f32[8,128,128]{2,1,0:T(8,128)} %pot_ref.1) | copy-start | bytes 1572868
  26.1 3.5 %copy-start.2 = (bf16[2,256,256]{2,1,0:T(8,128)(2,1)S(1)}, bf16[2,256,256]{2,1,0:T(8,128)(2,1)}, u32[]{:S(2)}) copy-start(bf16[2,256,256]{2,1,0:T(8,128)(2,1)} %constant.72.clone.byl_ref) | copy-start | bytes 786436
  38.0 7.8 %copy-start.15 = (bf16[224,128]{1,0:T(8,128)(2,1)S(1)}, bf16[224,128]{1,0:T(8,128)(2,1)}, u32[]{:S(2)}) copy-start(bf16[224,128]{1,0:T(8,128)(2,1)} %get-tuple-element.10) | copy-start | bytes 172036
  38.0 19.8 %all-to-all-start.1 = ((s16[16,16,256]{2,1,0:T(8,128)(2,1)}), s16[16,16,256]{2,1,0:T(8,128)(2,1)S(1)}, u32[]{:S(2)}, u32[]{:S(2)}) async-start(s16[16,16,256]{2,1,0:T(8,128)(2,1)} %shard_map.168), calls=%async_computation.1 | async-start | bytes 262144 | tf_op jit(solution)/shard_map/all_to_all | solution.py:376
  45.8 12.0 %copy-start.9 = (bf16[256,256]{1,0:T(8,128)(2,1)S(1)}, bf16[256,256]{1,0:T(8,128)(2,1)}, u32[]{:S(2)}) copy-start(bf16[256,256]{1,0:T(8,128)(2,1)} %constant.73.clone.high_ref) | copy-start | bytes 393220
  45.8 12.0 %copy-start.10 = (f32[256,8]{1,0:T(8,128)S(1)}, f32[256,8]{1,0:T(8,128)}, u32[]{:S(2)}) copy-start(f32[256,8]{1,0:T(8,128)} %get-tuple-element.12.cols_ref) | copy-start | bytes 24580
  45.8 12.0 %copy-start = (f32[2,1,224,128]{3,2,1,0:T(8,128)S(1)}, f32[2,1,224,128]{3,2,1,0:T(8,128)}, u32[]{:S(2)}) copy-start(f32[2,1,224,128]{3,2,1,0:T(8,128)} %orb_ref.1) | copy-start | bytes 688132
  45.8 12.0 %copy-start.8 = (bf16[256,256]{1,0:T(8,128)(2,1)S(1)}, bf16[256,256]{1,0:T(8,128)(2,1)}, u32[]{:S(2)}) copy-start(bf16[256,256]{1,0:T(8,128)(2,1)} %constant.74.clone.low_ref) | copy-start | bytes 393220
  45.8 6.7 %collective-permute-start.1 = (bf16[1,2,224,128]{3,2,1,0:T(8,128)(2,1)S(1)}, bf16[1,2,224,128]{3,2,1,0:T(8,128)(2,1)S(1)}, u32[]{:S(2)}, u32[]{:S(2)}) collective-permute-start(bf16[1,2,224,128]{3,2,1,0:T(8,128)(2,1)S(1)} %maximum_bitcast_fusion), channel_id=1, source_target_pairs={{0,4},{4,0},{8,12},{12,8},{1,5},{5,1},{9,13},{13,9},{2,6},{6,2},{1... | collective-permute-start | bytes 344072 | tf_op jit(solution)/shard_map/ppermute | solution.py:373
  52.6 10.5 %collective-permute-start.2 = (bf16[2,2,224,128]{3,2,1,0:T(8,128)(2,1)S(1)}, bf16[2,2,224,128]{3,2,1,0:T(8,128)(2,1)S(1)}, u32[]{:S(2)}, u32[]{:S(2)}) collective-permute-start(bf16[2,2,224,128]{3,2,1,0:T(8,128)(2,1)S(1)} %pad_maximum_fusion.1), channel_id=1, source_target_pairs={{0,12},{4,8},{8,4},{12,0},{1,13},{5,9},{9,5},{13,1},{2,14},{6,10},... | collective-permute-start | bytes 688136 | tf_op jit(solution)/shard_map/ppermute | solution.py:374
  59.1 11.6 %all-to-all-start.2 = ((bf16[4,2,224,128]{3,2,1,0:T(8,128)(2,1)}), bf16[4,2,224,128]{3,2,1,0:T(8,128)(2,1)S(1)}, u32[]{:S(2)}, u32[]{:S(2)}) async-start(bf16[4,2,224,128]{3,2,1,0:T(8,128)(2,1)} %get-tuple-element.15), calls=%async_computation.2 | async-start | bytes 917504 | tf_op jit(solution)/shard_map/all_to_all | solution.py:380

commit v3 on v2

--- a/solution.py
+++ b/solution.py
@@ -25,6 +25,7 @@
 BF16 = jnp.bfloat16
 FULL = ("zlo", "core", "zhi", "y", "x")
 VMEM = 48 * 1024 * 1024
+WHOLE = 62 * 1024 * 1024
 
 
 def halves(table):
@@ -152,45 +153,43 @@
     out_ref[...] = encode(out.reshape(FFT, 2 * PLANES, PAD))
 
 
-def plane_kernel(
-    val_ref,
-    group_ref,
-    col_ref,
-    colt_ref,
-    pot_ref,
-    yh_ref,
-    yl_ref,
-    xh_ref,
-    xl_ref,
-    bxh_ref,
-    bxl_ref,
-    byh_ref,
-    byl_ref,
-    out_ref,
-    spread_ref,
-    hot_ref,
-    t_ref,
-    g_ref,
-):
+def places(coords_ref, half_ref):
+    gx, gy = coords_ref[0:1, :], coords_ref[1:2, :]
+    half = jnp.concatenate([half_ref[i : i + 1, :] for i in range(half_ref.shape[0])], axis=1)
+    edge = gy == RADIUS
+    v = jnp.where(edge, 2 * RADIUS + 1, gx + RADIUS)
+    u = jnp.where(edge, 0, gy + RADIUS)
+    cell = jnp.where(half >= 0, (v // 4) * 256 + (v % 4) * 64 + u, -256)
+    cell = jnp.concatenate([cell, jnp.full((1, PAD - OWN), -256, jnp.int32)], axis=1)
+    cell = jnp.concatenate([cell[:, c * OWN : c * OWN + PAD] for c in range(FFT)], axis=0)
+    lane = lax.broadcasted_iota(jnp.int32, cell.shape, 1)
+    cell = jnp.where(lane < OWN, cell, -256)
+    return cell >> 8, cell & 255
+
+
+def plane_kernel(val_ref, coords_ref, half_ref, pot_ref, yh, yl, xh, xl, bxh, bxl, byh, byl, out_ref, spread_ref, t_ref, g_ref):
     block = 2 * PLANES
+    group, col = places(coords_ref, half_ref)
     values = decode(val_ref[...])
+    sub = lax.broadcasted_iota(jnp.int32, (256, PAD), 0)
+    hots = [jnp.where(sub == col[c : c + 1], 1.0, 0.0).astype(BF16) for c in range(FFT)]
     for c in range(FFT):
         value = values[c]
         high = value.astype(BF16).astype(F32)
         low = value - high
-        group = group_ref[c : c + 1, :]
         for r in range(GROUPS):
-            here = jnp.broadcast_to(group == r, (block, PAD))
+            here = jnp.broadcast_to(group[c : c + 1] == r, (block, PAD))
             spread_ref[r * block : (r + 1) * block, c * PAD : (c + 1) * PAD] = jnp.where(here, high, 0.0).astype(BF16)
             spread_ref[ROWS + r * block : ROWS + (r + 1) * block, c * PAD : (c + 1) * PAD] = jnp.where(here, low, 0.0).astype(BF16)
-        lane = lax.broadcasted_iota(jnp.int32, (PAD, 256), 1)
-        hot_ref[c * PAD : (c + 1) * PAD, :] = jnp.where(lane == colt_ref[:, c : c + 1], 1.0, 0.0).astype(BF16)
-    window = dot(spread_ref[...], hot_ref[...])
+    window = lax.dot_general(
+        jnp.concatenate(hots, axis=1), spread_ref[...], (((1,), (1,)), ((), ())), preferred_element_type=F32
+    )
+    window = jnp.transpose(window)
     window = window[:ROWS] + window[ROWS:]
 
     quarter = lax.broadcasted_iota(jnp.int32, (ROWS, 256), 1) // 64
     stacked = jnp.concatenate([jnp.where(quarter == q, window, 0.0) for q in range(4)], axis=0)
-    along = dot3(split(stacked), (yh_ref[...], yl_ref[...]))
+    along = dot3(split(stacked), (yh[...], yl[...]))
     along = along.reshape(4, GROUPS, 2, PLANES, 256)
     real = along[:, :, 0, :, :GRID] - along[:, :, 1, :, GRID:]
     imag = along[:, :, 0, :, GRID:] + along[:, :, 1, :, :GRID]
@@ -209,10 +208,10 @@
         p = 2 * pair
         planes = [t_ref[pl.ds(p + i, count, stride=PLANES), :] for i in range(2)]
         part = jnp.concatenate([jnp.concatenate(planes, axis=1), fill], axis=0)
-        field = dot3((xh_ref[...], xl_ref[...]), split(part))
+        field = dot3((xh[...], xl[...]), split(part))
         pot = jnp.concatenate([pot_ref[p], pot_ref[p + 1]], axis=1)
         field = field * jnp.concatenate([pot, pot], axis=0)
-        back = dot3((bxh_ref[...], bxl_ref[...]), split(field))
+        back = dot3((bxh[...], bxl[...]), split(field))
         for i in range(2):
             g_ref[pl.ds(p + i, count, stride=PLANES), :] = back[:count, i * GRID : (i + 1) * GRID]
     for base in (special, half + special):
@@ -223,24 +222,21 @@
     rows = GROUPS * PLANES
     quarter = lax.broadcasted_iota(jnp.int32, (rows, 256), 1) // 64
     for i in range(2):
-        cells = dot3(couple, (byh_ref[i], byl_ref[i]))
-        total = jnp.zeros((rows, 256), F32)
-        for q in range(4):
+        cells = dot3(couple, (byh[i], byl[i]))
+        total = cells[:rows]
+        for q in range(1, 4):
             total = jnp.where(quarter == q, cells[q * rows : (q + 1) * rows], total)
         parts.append(total.reshape(GROUPS, 1, PLANES, 256))
     cells = jnp.concatenate(parts, axis=1).reshape(ROWS, 256)
     high, low = split(cells)
     cells = jnp.concatenate([high, low], axis=0)
 
-    sub = lax.broadcasted_iota(jnp.int32, (256, PAD), 0)
     for c in range(FFT):
-        hot = jnp.where(sub == col_ref[c : c + 1, :], 1.0, 0.0).astype(BF16)
-        found = dot(cells, hot)
+        found = dot(cells, hots[c])
         found = found[:ROWS] + found[ROWS:]
-        group = group_ref[c : c + 1, :]
         total = jnp.zeros((block, PAD), F32)
         for r in range(GROUPS):
-            here = jnp.broadcast_to(group == r, (block, PAD))
+            here = jnp.broadcast_to(group[c : c + 1] == r, (block, PAD))
             total = jnp.where(here, found[r * block : (r + 1) * block], total)
         out_ref[c : c + 1] = encode(total[None])
 
@@ -262,8 +258,7 @@
 
 
 def block_kernel(left_ref, pair_ref, out_ref, sums_ref, second_ref):
-    depth, sides = left_ref.shape[0], left_ref.shape[1]
-    width = pair_ref.shape[0]
+    sides, depth, width = 2, 4, pair_ref.shape[0]
     lane = lax.broadcasted_iota(jnp.int32, (OWN, SLOTS), 1)
     sign = jnp.where(lane < 64, 1.0, -1.0)
     side, y = lax.axis_index("zhi"), lax.axis_index("y")
@@ -273,20 +268,18 @@
             second = pair_ref[x, m].astype(F32)
             second_ref[2 * m] = second
             second_ref[2 * m + 1] = pltpu.roll(second, 64, 1) * sign
-
-        def one(j, carry):
-            order, other = j // sides, lax.rem(j, sides)
-            mine = left_ref[order, other].astype(F32)
-            flip = lax.rem(order, 2)
-            near = y + flip * (1 - 2 * lax.rem(y, 2))
-            row = jnp.where(order >= 2, depth - 1 - near, near) + depth * lax.rem(side + other, sides)
+        for order in range(depth):
+            mine = [left_ref[order * sides + other].astype(F32) for other in range(sides)]
+            near = y + (order % 2) * (1 - 2 * lax.rem(y, 2))
+            line = depth - 1 - near if order >= 2 else near
             for t in range(4):
-                product = (mine * second_ref[t]).reshape(OWN // 8, 8, SLOTS)
-                place = (t * sides * depth + row) * width + x
-                sums_ref[pl.ds(pl.multiple_of(place * 8, 8), 8), :] = jnp.sum(product, axis=0)
-            return carry
-
-        return lax.fori_loop(0, depth * sides, one, carry)
+                second = second_ref[t]
+                for other in range(sides):
+                    product = (mine[other] * second).reshape(OWN // 8, 8, SLOTS)
+                    row = line + depth * lax.rem(side + other, sides)
+                    place = (t * sides * depth + row) * width + x
+                    sums_ref[pl.ds(pl.multiple_of(place * 8, 8), 8), :] = jnp.sum(product, axis=0)
+        return carry
 
     lax.fori_loop(0, width, column, 0)
     total = jnp.sum(sums_ref[...].reshape(-1, 8, SLOTS), axis=1)
@@ -297,11 +290,30 @@
     out_ref[...] = summed * (1.0 / RADIUS**3)
 
 
-def call(kernel, out_shape, count, scratch=(), flops=10**8, traffic=10**6, hbm=False, limit=VMEM):
+def matrix_kernel(columns_ref, out_ref):
+    depth = width = 4
+    sides = columns_ref.shape[1]
+    lane = lax.broadcasted_iota(jnp.int32, (depth * sides, SLOTS), 1) % width
+    rows = []
+    for x in range(width):
+        rows.append(jnp.concatenate([columns_ref[y * width + x] for y in range(depth)], axis=0))
+    bands = []
+    for right in range(width):
+        merged = rows[right]
+        for x in range(width):
+            if x != right:
+                merged = jnp.where(lane == x, pltpu.roll(rows[x], (x - right) % SLOTS, 1), merged)
+        bands.append(merged)
+    order = [(side, y, x) for side in range(sides) for y in range(depth) for x in range(width)]
+    columns = jnp.concatenate([bands[x][y * sides + side : y * sides + side + 1] for side, y, x in order], axis=0)
+    out_ref[...] = jnp.transpose(columns)
+
+
+def call(kernel, out_shape, count, scratch=(), flops=10**8, traffic=10**6, hbm=(), limit=VMEM):
     return pl.pallas_call(
         kernel,
         out_shape=out_shape,
-        in_specs=[pl.BlockSpec(memory_space=pl.ANY if hbm else pltpu.VMEM)] * count,
+        in_specs=[pl.BlockSpec(memory_space=pl.ANY if i in hbm else pltpu.VMEM) for i in range(count)],
         scratch_shapes=list(scratch),
         compiler_params=pltpu.CompilerParams(vmem_limit_bytes=limit),
         cost_estimate=pl.CostEstimate(flops=flops, bytes_accessed=traffic, transcendentals=0),
@@ -309,10 +321,9 @@
 
 
 def solution(mesh):
-    fft, band = mesh.shape["fft"], mesh.shape["band"]
-    shape = (fft // 2, 2) + ((2, 4, 4) if band == 32 else (1, 1, band))
-    fine = Mesh(mesh.devices.reshape(shape), FULL)
-    sides, depth, width = shape[2:]
+    fft = mesh.shape["fft"]
+    sides, depth, width = 2, 4, 4
+    fine = Mesh(mesh.devices.reshape(fft // 2, 2, sides, depth, width), FULL)
     groups = depth * width
     bands = sides * groups
     shaped = jax.ShapeDtypeStruct
@@ -323,7 +334,7 @@
     byh, byl = halves(y_back_table())
 
     def local(orbitals, potential, stick_coords, stick_half):
-        gx, gy = stick_coords[0], stick_coords[1]
+        halves_of = stick_half.reshape(28, 128)
         stick = (OWN, SLOTS)
         sent, left, cols = call(
             z_kernel,
@@ -337,41 +348,32 @@
                 pltpu.VMEM((28, 128), jnp.int32),
                 pltpu.SemaphoreType.DMA((5,)),
             ],
-            hbm=True,
-            limit=62 * 1024 * 1024,
-        )(orbitals, zh, zl, stick_coords, stick_half.reshape(28, 128))
+            flops=5 * 10**10,
+            traffic=10**8,
+            hbm=range(5),
+            limit=WHOLE,
+        )(orbitals, zh, zl, stick_coords, halves_of)
         received = lax.all_to_all(sent, ("zlo", "core"), 0, 0, tiled=True)
-
-        edge = gy == RADIUS
-        v = jnp.where(edge, 2 * RADIUS + 1, gx + RADIUS)
-        u = jnp.where(edge, 0, gy + RADIUS)
-        group = jnp.where(stick_half >= 0, v // 4, -1)
-        col = (v % 4) * 64 + u
-        group = jnp.pad(group.reshape(FFT, OWN), ((0, 0), (0, PAD - OWN)), constant_values=-1)
-        col = jnp.pad(col.reshape(FFT, OWN), ((0, 0), (0, PAD - OWN)))
 
         picked = call(
             plane_kernel,
             shaped((FFT, 2 * PLANES, PAD), jnp.int16),
-            13,
+            12,
             scratch=[
                 pltpu.VMEM((2 * ROWS, FFT * PAD), BF16),
-                pltpu.VMEM((FFT * PAD, 256), BF16),
                 pltpu.VMEM((2 * 4 * GROUPS * PLANES, GRID), F32),
                 pltpu.VMEM((2 * 4 * GROUPS * PLANES, GRID), F32),
             ],
             flops=1,
             traffic=1,
-        )(received, group, col, col.T, potential, yh, yl, xh, xl, xh.T, xl.T, byh, byl)
-        lefts = left[None]
-        if sides > 1:
-            far = lax.ppermute(left, "zhi", [(0, 1), (1, 0)])
-            picked, far = lax.optimization_barrier((picked, far))
-            lefts = jnp.stack([left, far])
-        lefts = lefts[None]
-        if depth > 1:
-            lefts = jnp.concatenate([lefts, lax.ppermute(lefts, "y", [(i, i ^ 1) for i in range(depth)])])
-            lefts = jnp.concatenate([lefts, lax.ppermute(lefts, "y", [(i, depth - 1 - i) for i in range(depth)])])
+        )(received, stick_coords, halves_of, potential, yh, yl, xh, xl, xh.T, xl.T, byh, byl)
+
+        far = lax.ppermute(left, "zhi", [(0, 1), (1, 0)])
+        picked, far = lax.optimization_barrier((picked, far))
+        lefts = jnp.stack([left, far])
+        beside = lax.ppermute(lefts, "y", [(i, i ^ 1) for i in range(depth)])
+        lefts = jnp.concatenate([lefts, beside])
+        lefts = jnp.concatenate([lefts, lax.ppermute(lefts, "y", [(i, depth - 1 - i) for i in range(depth)])])
 
         mixed = lax.all_to_all(picked, ("zlo", "core"), 0, 0, tiled=True)
         applied, spread = call(apply_kernel, [shaped(orbitals.shape, F32), shaped((width, 2) + stick, BF16)], 5)(
@@ -389,8 +391,8 @@
         column = jnp.sum(column.reshape(fft, sides, 4 * bands), axis=0)
         column = jnp.broadcast_to(column[None], (groups, sides, 4 * bands))
         columns = lax.all_to_all(column, ("y", "x"), 0, 0, tiled=True)
-        columns = columns.reshape(depth, width, sides, 4, sides, depth, width)
-        subspace = jnp.transpose(columns, (3, 4, 5, 1, 2, 0, 6)).reshape(2, 2, bands, bands)
+        subspace = call(matrix_kernel, shaped((4 * bands, bands), F32), 1)(columns)
+        subspace = subspace.reshape(2, 2, bands, bands)
         return applied, subspace
 
     across = ("zhi", "y", "x")

time: 107 us -> 105 us (0.981)
  local copies, waits for them, and re-layouts: 2.66 us -> 0.15 us
    reshape x3 -> x0, local copies, waits for them, and re-layouts: 1.74 us -> none  [the longest x1 0.98 us: local(): jnp.transpose(columns, (3, 4, 5, 1, 2, 0, 6)).reshape(2, 2, bands, bands)]
    pallas_call x1 -> x2, Pallas kernels: 8.35 us -> 8.13 us  [the longest x1 7.32 us: local(): call(plane_kernel, shaped((FFT, 2 * PLANES, PAD), jnp.int16), 12, scratch...]
  transfers between devices with their start and end apart: 6 -> 6, of which waited for: 4 -> 4; matrix products, arithmetic and copies ran while one was open for 1% -> 0% of each run, Pallas kernels for 9% -> 8%
where the time goes in v3:
time: 105 us
  starting transfers between devices  42 us (40%)
  blocking collectives  32.5 us (31%)
  waiting for transfers between devices  15.5 us (15%)
  Pallas kernels  13.6 us (13%)
    all_to_all x1, blocking collectives, local(): column = lax.all_to_all(column, ('zlo', 'core', 'zhi'), 0, 0, tiled=True)  22.5 us
    all_to_all x1, starting transfers between devices, local(): received = lax.all_to_all(sent, ('zlo', 'core'), 0, 0, tiled=True)  14.2 us
    all_to_all x1, blocking collectives, local(): columns = lax.all_to_all(column, ('y', 'x'), 0, 0, tiled=True)  10 us
    ppermute x1, starting transfers between devices, local(): far = lax.ppermute(left, 'zhi', [(0, 1), (1, 0)])  7.96 us
    all_to_all x1, starting transfers between devices, local(): mixed = lax.all_to_all(picked, ('zlo', 'core'), 0, 0, tiled=True)  7.87 us
    all_to_all x1, waiting for transfers between devices, local(): pairs = lax.all_to_all(spread, 'x', 0, 0, tiled=True)  7.55 us
    pallas_call x1, Pallas kernels, local(): call(plane_kernel, shaped((FFT, 2 * PLANES, PAD), jnp.int16), 12, scratch...  7.32 us
    ppermute x1, starting transfers between devices, local(): lax.ppermute(lefts, 'y', [(i, depth - 1 - i) for i in range(depth)])  4.64 us
  transfers between devices with their start and end apart: 6, of which 4 were waited for; matrix products, arithmetic and copies ran while one was open for 0% of the time, Pallas kernels for 8%

profile of v3, /device:TPU:1, one launch (start us, length us, event | category | flops | bytes accessed | tf_op | source)
XLA Modules:
  0.0 104.8 jit_solution(5043440653458482749)
XLA Ops:
  0.6 0.0 copy-start.2
  0.7 0.0 copy-start.4
  0.7 0.0 copy-start.5
  0.7 0.0 copy-start.6
  0.7 0.0 copy-start.7
  0.7 0.0 copy-start.11
  0.7 0.0 copy-start.12
  0.7 2.7 %shard_map.167 = (s16[16,16,256]{2,1,0:T(8,128)(2,1)}, bf16[224,128]{1,0:T(8,128)(2,1)}, f32[256,8]{1,0:T(8,128)}) custom-call(f32[2,1,224,128]{3,2,1,0:T(8,128)} %orb_ref.1, bf16[256,256]{1,0:T(8,128)(2,1)} %constant.26.clone.high_hbm, bf16[256,256]{1,0:T(8,128)(2,1)} %constant.27.clone.low_hbm, s32[2,3584]{1,0:T(2,128)} %coords_ref.1, s32[28,128]{1,0:T(8,128)} %bitcast.7), custom_call_target="tpu_custom_call" | custom-call | flops 49999998976 | bytes 100000000 | tf_op jit(solution)/shard_map/pallas_call | solution.py:339
  3.4 0.0 copy-start.1
  3.4 14.2 %all-to-all-start = ((s16[16,16,256]{2,1,0:T(8,128)(2,1)}), s16[16,16,256]{2,1,0:T(8,128)(2,1)S(1)}, u32[]{:S(2)}, u32[]{:S(2)}) async-start(s16[16,16,256]{2,1,0:T(8,128)(2,1)} %get-tuple-element.9), calls=%async_computation | async-start | bytes 262144 | tf_op jit(solution)/shard_map/all_to_all | solution.py:356
  17.6 8.0 %collective-permute-start = (bf16[224,128]{1,0:T(8,128)(2,1)}, bf16[224,128]{1,0:T(8,128)(2,1)S(1)}, u32[]{:S(2)}, u32[]{:S(2)}) collective-permute-start(bf16[224,128]{1,0:T(8,128)(2,1)} %get-tuple-element.10), channel_id=1, source_target_pairs={{0,16},{16,0},{1,17},{17,1},{2,18},{18,2},{3,19},{19,3},{4,20},{20... | collective-permute-start | bytes 172040 | tf_op jit(solution)/shard_map/ppermute | solution.py:371
  25.6 4.1 %all-to-all-done.val_ref = s16[16,16,256]{2,1,0:T(8,128)(2,1)S(1)} async-done(((s16[16,16,256]{2,1,0:T(8,128)(2,1)}), s16[16,16,256]{2,1,0:T(8,128)(2,1)S(1)}, u32[]{:S(2)}, u32[]{:S(2)}) %all-to-all-start) | async-done | bytes 131104 | tf_op jit(solution)/shard_map/all_to_all | solution.py:356
  29.6 0.0 copy-done.2
  29.7 7.3 %shard_map.168 = s16[16,16,256]{2,1,0:T(8,128)(2,1)} custom-call(s16[16,16,256]{2,1,0:T(8,128)(2,1)S(1)} %all-to-all-done.val_ref, s32[2,3584]{1,0:T(2,128)S(1)} %copy-done.13, s32[28,128]{1,0:T(8,128)S(1)} %bitcast.8, f32[8,128,128]{2,1,0:T(8,128)S(1)} %copy-done, bf16[256,256]{1,0:T(8,128)(2,1)S(1)} %copy-done.7, bf16[256,256]{1,0:T(8,128)(2,1)S(1)} %copy-done.6, ...), custom_call_target="tpu_custom_call" | custom-call | flops 1 | bytes 1 | tf_op jit(solution)/shard_map/pallas_call | solution.py:358
  37.0 0.0 collective-permute-done
  37.1 7.9 %all-to-all-start.1 = ((s16[16,16,256]{2,1,0:T(8,128)(2,1)}), s16[16,16,256]{2,1,0:T(8,128)(2,1)S(1)}, u32[]{:S(2)}, u32[]{:S(2)}) async-start(s16[16,16,256]{2,1,0:T(8,128)(2,1)} %shard_map.168), calls=%async_computation.1 | async-start | bytes 262144 | tf_op jit(solution)/shard_map/all_to_all | solution.py:378
  44.9 0.0 copy-start.9
  45.0 0.0 copy-start.3
  45.0 0.0 copy-start.8
  45.0 3.4 %collective-permute-start.1 = (bf16[2,224,128]{2,1,0:T(8,128)(2,1)S(1)}, bf16[2,224,128]{2,1,0:T(8,128)(2,1)S(1)}, u32[]{:S(2)}, u32[]{:S(2)}) collective-permute-start(bf16[2,224,128]{2,1,0:T(8,128)(2,1)S(1)} %pad_maximum_fusion.2), channel_id=1, source_target_pairs={{0,4},{4,0},{8,12},{12,8},{1,5},{5,1},{9,13},{13,9},{2,6},{6,2},{1... | collective-permute-start | bytes 344072 | tf_op jit(solution)/shard_map/ppermute | solution.py:374
  48.4 3.4 %collective-permute-done.1 = bf16[2,224,128]{2,1,0:T(8,128)(2,1)S(1)} collective-permute-done((bf16[2,224,128]{2,1,0:T(8,128)(2,1)S(1)}, bf16[2,224,128]{2,1,0:T(8,128)(2,1)S(1)}, u32[]{:S(2)}, u32[]{:S(2)}) %collective-permute-start.1) | collective-permute-done | bytes 114720 | tf_op jit(solution)/shard_map/ppermute | solution.py:374
  51.8 4.6 %collective-permute-start.2 = (bf16[4,224,128]{2,1,0:T(8,128)(2,1)S(1)}, bf16[4,224,128]{2,1,0:T(8,128)(2,1)S(1)}, u32[]{:S(2)}, u32[]{:S(2)}) collective-permute-start(bf16[4,224,128]{2,1,0:T(8,128)(2,1)S(1)} %pad_maximum_fusion.1), channel_id=1, source_target_pairs={{0,12},{4,8},{8,4},{12,0},{1,13},{5,9},{9,5},{13,1},{2,14},{6,10},... | collective-permute-start | bytes 688136 | tf_op jit(solution)/shard_map/ppermute | solution.py:376
  56.4 0.5 all-to-all-done.1.mix_ref
  56.9 0.0 copy-done.10
  57.0 1.3 %shard_map.169 = (f32[2,1,224,128]{3,2,1,0:T(8,128)}, bf16[4,2,224,128]{3,2,1,0:T(8,128)(2,1)}) custom-call(s16[16,16,256]{2,1,0:T(8,128)(2,1)S(1)} %all-to-all-done.1.mix_ref, f32[2,1,224,128]{3,2,1,0:T(8,128)S(1)} %copy-done.3, f32[256,8]{1,0:T(8,128)S(1)} %copy-done.10, bf16[256,256]{1,0:T(8,128)(2,1)S(1)} %copy-done.9, bf16[256,256]{1,0:T(8,128)(2,1)S(1)} %copy-done.8), custom_call_target="tpu_custom_call" | custom-call | flops 100000000 | bytes 1000000 | tf_op jit(solution)/shard_map/pallas_call | solution.py:379
  58.3 4.0 %all-to-all-start.2 = ((bf16[4,2,224,128]{3,2,1,0:T(8,128)(2,1)}), bf16[4,2,224,128]{3,2,1,0:T(8,128)(2,1)S(1)}, u32[]{:S(2)}, u32[]{:S(2)}) async-start(bf16[4,2,224,128]{3,2,1,0:T(8,128)(2,1)} %get-tuple-element.15), calls=%async_computation.2 | async-start | bytes 917504 | tf_op jit(solution)/shard_map/all_to_all | solution.py:382
  62.3 0.0 collective-permute-done.2
  62.3 7.5 %all-to-all-done.2.pair_ref = bf16[4,2,224,128]{3,2,1,0:T(8,128)(2,1)S(1)} async-done(((bf16[4,2,224,128]{3,2,1,0:T(8,128)(2,1)}), bf16[4,2,224,128]{3,2,1,0:T(8,128)(2,1)S(1)}, u32[]{:S(2)}, u32[]{:S(2)}) %all-to-all-start.2) | async-done | bytes 458784 | tf_op jit(solution)/shard_map/all_to_all | solution.py:382
  69.9 1.5 %shard_map.170 = f32[8,128]{1,0:T(8,128)S(1)} custom-call(bf16[8,224,128]{2,1,0:T(8,128)(2,1)S(1)} %pad_maximum_fusion.left_ref, bf16[4,2,224,128]{3,2,1,0:T(8,128)(2,1)S(1)} %all-to-all-done.2.pair_ref), custom_call_target="tpu_custom_call" | custom-call | flops 100000000 | bytes 1000000 | tf_op jit(solution)/shard_map/pallas_call | solution.py:383
  71.5 22.5 %all_to_all.25 = f32[32,1,128]{2,1,0:T(1,128)S(1)} all-to-all(f32[32,1,128]{2,1,0:T(1,128)S(1)} %broadcast_in_dim.7), channel_id=1, replica_groups=mesh['zlo'=8,'core'=2,'zhi'=2,'y'=4,'x'=4] {'zlo','core','zhi'}, dimensions={0} | all-to-all | bytes 32768 | tf_op jit(solution)/shard_map/all_to_all | solution.py:390
  94.0 10.0 %all_to_all.26.columns_ref = f32[16,2,128]{2,1,0:T(2,128)S(1)} all-to-all(f32[16,2,128]{2,1,0:T(2,128)S(1)} %broadcast_in_dim.16), channel_id=1, replica_groups=mesh['zlo'=8,'core'=2,'zhi'=2,'y'=4,'x'=4] {'y','x'}, dimensions={0} | all-to-all | bytes 32768 | tf_op jit(solution)/shard_map/all_to_all | solution.py:393
  104.0 0.8 shard_map.171
  (26 shorter events, 0.2 us)
Async XLA Ops:
  0.6 29.0 %copy-start = (f32[8,128,128]{2,1,0:T(8,128)S(1)}, f32[8,128,128]{2,1,0:T(8,128)}, u32[]{:S(2)}) copy-start(f32[8,128,128]{2,1,0:T(8,128)} %pot_ref.1) | copy-start | bytes 1572868
  0.6 29.0 %copy-start.2 = (bf16[2,256,256]{2,1,0:T(8,128)(2,1)S(1)}, bf16[2,256,256]{2,1,0:T(8,128)(2,1)}, u32[]{:S(2)}) copy-start(bf16[2,256,256]{2,1,0:T(8,128)(2,1)} %constant.34.clone.byh) | copy-start | bytes 786436
  0.7 29.0 %copy-start.4 = (bf16[256,144]{1,0:T(8,128)(2,1)S(1)}, bf16[256,144]{1,0:T(8,128)(2,1)}, u32[]{:S(2)}) copy-start(bf16[256,144]{1,0:T(8,128)(2,1)} %constant.31.clone.xl) | copy-start | bytes 221188
  0.7 29.0 %copy-start.5 = (bf16[256,144]{1,0:T(8,128)(2,1)S(1)}, bf16[256,144]{1,0:T(8,128)(2,1)}, u32[]{:S(2)}) copy-start(bf16[256,144]{1,0:T(8,128)(2,1)} %constant.30.clone.xh) | copy-start | bytes 221188
  0.7 29.0 %copy-start.6 = (bf16[256,256]{1,0:T(8,128)(2,1)S(1)}, bf16[256,256]{1,0:T(8,128)(2,1)}, u32[]{:S(2)}) copy-start(bf16[256,256]{1,0:T(8,128)(2,1)} %constant.29.clone.yl) | copy-start | bytes 393220
  0.7 29.0 %copy-start.7 = (bf16[256,256]{1,0:T(8,128)(2,1)S(1)}, bf16[256,256]{1,0:T(8,128)(2,1)}, u32[]{:S(2)}) copy-start(bf16[256,256]{1,0:T(8,128)(2,1)} %constant.28.clone.yh) | copy-start | bytes 393220
  0.7 29.0 %copy-start.11 = (bf16[144,256]{1,0:T(8,128)(2,1)S(1)}, bf16[144,256]{1,0:T(8,128)(2,1)}, u32[]{:S(2)}) copy-start(bf16[144,256]{1,0:T(8,128)(2,1)} %constant.33.clone.bxl) | copy-start | bytes 221188
  0.7 29.0 %copy-start.12 = (bf16[144,256]{1,0:T(8,128)(2,1)S(1)}, bf16[144,256]{1,0:T(8,128)(2,1)}, u32[]{:S(2)}) copy-start(bf16[144,256]{1,0:T(8,128)(2,1)} %constant.32.clone.bxh) | copy-start | bytes 221188
  0.7 29.0 %copy-start.13 = (s32[2,3584]{1,0:T(2,128)S(1)}, s32[2,3584]{1,0:T(2,128)}, u32[]{:S(2)}) copy-start(s32[2,3584]{1,0:T(2,128)} %coords_ref.1) | copy-start | bytes 86020
  0.7 29.0 %copy-start.14 = (s32[3584]{0:T(1024)S(1)}, s32[3584]{0:T(1024)}, u32[]{:S(2)}) copy-start(s32[3584]{0:T(1024)} %param.19) | copy-start | bytes 43012
  3.4 26.3 %copy-start.1 = (bf16[2,256,256]{2,1,0:T(8,128)(2,1)S(1)}, bf16[2,256,256]{2,1,0:T(8,128)(2,1)}, u32[]{:S(2)}) copy-start(bf16[2,256,256]{2,1,0:T(8,128)(2,1)} %constant.35.clone.byl) | copy-start | bytes 786436
  3.4 26.2 %all-to-all-start = ((s16[16,16,256]{2,1,0:T(8,128)(2,1)}), s16[16,16,256]{2,1,0:T(8,128)(2,1)S(1)}, u32[]{:S(2)}, u32[]{:S(2)}) async-start(s16[16,16,256]{2,1,0:T(8,128)(2,1)} %get-tuple-element.9), calls=%async_computation | async-start | bytes 262144 | tf_op jit(solution)/shard_map/all_to_all | solution.py:356
  17.6 19.4 %collective-permute-start = (bf16[224,128]{1,0:T(8,128)(2,1)}, bf16[224,128]{1,0:T(8,128)(2,1)S(1)}, u32[]{:S(2)}, u32[]{:S(2)}) collective-permute-start(bf16[224,128]{1,0:T(8,128)(2,1)} %get-tuple-element.10), channel_id=1, source_target_pairs={{0,16},{16,0},{1,17},{17,1},{2,18},{18,2},{3,19},{19,3},{4,20},{20... | collective-permute-start | bytes 172040 | tf_op jit(solution)/shard_map/ppermute | solution.py:371
  37.0 7.9 %copy-start.15 = (bf16[224,128]{1,0:T(8,128)(2,1)S(1)}, bf16[224,128]{1,0:T(8,128)(2,1)}, u32[]{:S(2)}) copy-start(bf16[224,128]{1,0:T(8,128)(2,1)} %get-tuple-element.10) | copy-start | bytes 172036
  37.1 19.9 %all-to-all-start.1 = ((s16[16,16,256]{2,1,0:T(8,128)(2,1)}), s16[16,16,256]{2,1,0:T(8,128)(2,1)S(1)}, u32[]{:S(2)}, u32[]{:S(2)}) async-start(s16[16,16,256]{2,1,0:T(8,128)(2,1)} %shard_map.168), calls=%async_computation.1 | async-start | bytes 262144 | tf_op jit(solution)/shard_map/all_to_all | solution.py:378
  44.9 12.0 %copy-start.9 = (bf16[256,256]{1,0:T(8,128)(2,1)S(1)}, bf16[256,256]{1,0:T(8,128)(2,1)}, u32[]{:S(2)}) copy-start(bf16[256,256]{1,0:T(8,128)(2,1)} %constant.36.clone.high_ref) | copy-start | bytes 393220
  44.9 12.0 %copy-start.10 = (f32[256,8]{1,0:T(8,128)S(1)}, f32[256,8]{1,0:T(8,128)}, u32[]{:S(2)}) copy-start(f32[256,8]{1,0:T(8,128)} %get-tuple-element.12.cols_ref) | copy-start | bytes 24580
  45.0 12.0 %copy-start.3 = (f32[2,1,224,128]{3,2,1,0:T(8,128)S(1)}, f32[2,1,224,128]{3,2,1,0:T(8,128)}, u32[]{:S(2)}) copy-start(f32[2,1,224,128]{3,2,1,0:T(8,128)} %orb_ref.1) | copy-start | bytes 688132
  45.0 12.0 %copy-start.8 = (bf16[256,256]{1,0:T(8,128)(2,1)S(1)}, bf16[256,256]{1,0:T(8,128)(2,1)}, u32[]{:S(2)}) copy-start(bf16[256,256]{1,0:T(8,128)(2,1)} %constant.37.clone.low_ref) | copy-start | bytes 393220
  45.0 6.7 %collective-permute-start.1 = (bf16[2,224,128]{2,1,0:T(8,128)(2,1)S(1)}, bf16[2,224,128]{2,1,0:T(8,128)(2,1)S(1)}, u32[]{:S(2)}, u32[]{:S(2)}) collective-permute-start(bf16[2,224,128]{2,1,0:T(8,128)(2,1)S(1)} %pad_maximum_fusion.2), channel_id=1, source_target_pairs={{0,4},{4,0},{8,12},{12,8},{1,5},{5,1},{9,13},{13,9},{2,6},{6,2},{1... | collective-permute-start | bytes 344072 | tf_op jit(solution)/shard_map/ppermute | solution.py:374
  51.8 10.5 %collective-permute-start.2 = (bf16[4,224,128]{2,1,0:T(8,128)(2,1)S(1)}, bf16[4,224,128]{2,1,0:T(8,128)(2,1)S(1)}, u32[]{:S(2)}, u32[]{:S(2)}) collective-permute-start(bf16[4,224,128]{2,1,0:T(8,128)(2,1)S(1)} %pad_maximum_fusion.1), channel_id=1, source_target_pairs={{0,12},{4,8},{8,4},{12,0},{1,13},{5,9},{9,5},{13,1},{2,14},{6,10},... | collective-permute-start | bytes 688136 | tf_op jit(solution)/shard_map/ppermute | solution.py:376
  58.3 11.6 %all-to-all-start.2 = ((bf16[4,2,224,128]{3,2,1,0:T(8,128)(2,1)}), bf16[4,2,224,128]{3,2,1,0:T(8,128)(2,1)S(1)}, u32[]{:S(2)}, u32[]{:S(2)}) async-start(bf16[4,2,224,128]{3,2,1,0:T(8,128)(2,1)} %get-tuple-element.15), calls=%async_computation.2 | async-start | bytes 917504 | tf_op jit(solution)/shard_map/all_to_all | solution.py:382

commit v4 on v3

--- a/solution.py
+++ b/solution.py
@@ -85,7 +85,7 @@
 
 def encode(value):
     top = jnp.max(jnp.max(jnp.abs(value), axis=1, keepdims=True), axis=2, keepdims=True)
-    power = jnp.floor(jnp.log2(jnp.maximum(top, 1e-30))) + 1.0
+    power = jnp.floor(jnp.log2(jnp.maximum(top, 1e-36))) + 1.0
     size = jnp.maximum(jnp.abs(value) * jnp.exp2(-power), 1e-30)
     size = jnp.minimum(jnp.exp2(jnp.log2(size) * (1.0 / 3.0)) * LEVELS + 0.5, LEVELS)
     size = jnp.floor(size)
@@ -96,7 +96,8 @@
 
 def decode(coded):
     coded = coded.astype(jnp.int32).astype(F32)
-    return coded * coded * coded * (jnp.exp2(coded[:, :, OWN : OWN + 1]) * (1.0 / LEVELS**3))
+    root = coded * (1.0 / LEVELS)
+    return root * root * root * jnp.exp2(coded[:, :, OWN : OWN + 1])
 
 
 def masked(orbitals, cols):
@@ -241,7 +242,7 @@
         out_ref[c : c + 1] = encode(total[None])
 
 
-def apply_kernel(mix_ref, orb_ref, cols_ref, high_ref, low_ref, applied_ref, spread_ref):
+def apply_kernel(mix_ref, orb_ref, left_ref, cols_ref, high_ref, low_ref, applied_ref, spread_ref):
     real, imag, valid, kinetic = masked(orb_ref, cols_ref[...])
     mixed = dot3((high_ref[...], low_ref[...]), split(decode(mix_ref[...]).reshape(256, PAD)))
     mixed_real = jnp.transpose(mixed[:SLOTS])[:OWN]
@@ -251,7 +252,7 @@
     applied_ref[0, 0] = applied_real
     applied_ref[1, 0] = applied_imag
     right = pack(applied_real, applied_imag).astype(BF16)
-    left = pack(real, imag).astype(BF16)
+    left = left_ref[...]
     for i in range(spread_ref.shape[0]):
         spread_ref[i, 0] = right
         spread_ref[i, 1] = left
@@ -376,8 +377,8 @@
         lefts = jnp.concatenate([lefts, lax.ppermute(lefts, "y", [(i, depth - 1 - i) for i in range(depth)])])
 
         mixed = lax.all_to_all(picked, ("zlo", "core"), 0, 0, tiled=True)
-        applied, spread = call(apply_kernel, [shaped(orbitals.shape, F32), shaped((width, 2) + stick, BF16)], 5)(
-            mixed, orbitals, cols, zh.T, zl.T
+        applied, spread = call(apply_kernel, [shaped(orbitals.shape, F32), shaped((width, 2) + stick, BF16)], 6)(
+            mixed, orbitals, left, cols, zh.T, zl.T
         )
         pairs = lax.all_to_all(spread, "x", 0, 0, tiled=True)
         column = call(

time: 105 us -> 105 us (level)
  no operation moved by 1% of the time
where the time goes in v4:
time: 105 us
  starting transfers between devices  41.8 us (40%)
  blocking collectives  32.5 us (31%)
  waiting for transfers between devices  15.5 us (15%)
  Pallas kernels  13.6 us (13%)
    all_to_all x1, blocking collectives, local(): column = lax.all_to_all(column, ('zlo', 'core', 'zhi'), 0, 0, tiled=True)  22.5 us
    all_to_all x1, starting transfers between devices, local(): received = lax.all_to_all(sent, ('zlo', 'core'), 0, 0, tiled=True)  14.2 us
    all_to_all x1, blocking collectives, local(): columns = lax.all_to_all(column, ('y', 'x'), 0, 0, tiled=True)  10 us
    ppermute x1, starting transfers between devices, local(): far = lax.ppermute(left, 'zhi', [(0, 1), (1, 0)])  7.96 us
    all_to_all x1, starting transfers between devices, local(): mixed = lax.all_to_all(picked, ('zlo', 'core'), 0, 0, tiled=True)  7.7 us
    all_to_all x1, waiting for transfers between devices, local(): pairs = lax.all_to_all(spread, 'x', 0, 0, tiled=True)  7.55 us
    pallas_call x1, Pallas kernels, local(): call(plane_kernel, shaped((FFT, 2 * PLANES, PAD), jnp.int16), 12, scratch...  7.3 us
    ppermute x1, starting transfers between devices, local(): lax.ppermute(lefts, 'y', [(i, depth - 1 - i) for i in range(depth)])  4.64 us
  transfers between devices with their start and end apart: 6, of which 4 were waited for; matrix products, arithmetic and copies ran while one was open for 0% of the time, Pallas kernels for 8%

profile of v4, /device:TPU:1, one launch (start us, length us, event | category | flops | bytes accessed | tf_op | source)
XLA Modules:
  0.0 104.6 jit_solution(14923171552769032898)
XLA Ops:
  0.6 0.0 copy-start.2
  0.7 0.0 copy-start.3
  0.7 0.0 copy-start.9
  0.7 0.0 copy-start.10
  0.7 0.0 copy-start.11
  0.7 0.0 copy-start.13
  0.7 2.7 %shard_map.167 = (s16[16,16,256]{2,1,0:T(8,128)(2,1)}, bf16[224,128]{1,0:T(8,128)(2,1)}, f32[256,8]{1,0:T(8,128)}) custom-call(f32[2,1,224,128]{3,2,1,0:T(8,128)} %orb_ref.1, bf16[256,256]{1,0:T(8,128)(2,1)} %constant.26.clone.high_hbm, bf16[256,256]{1,0:T(8,128)(2,1)} %constant.27.clone.low_hbm, s32[2,3584]{1,0:T(2,128)} %coords_ref.1, s32[28,128]{1,0:T(8,128)} %bitcast.10), custom_call_target="tpu_custom_call" | custom-call | flops 49999998976 | bytes 100000000 | tf_op jit(solution)/shard_map/pallas_call | solution.py:340
  3.4 0.0 copy-start
  3.4 0.0 copy-start.8
  3.4 0.0 copy-start.12
  3.4 14.2 %all-to-all-start = ((s16[16,16,256]{2,1,0:T(8,128)(2,1)}), s16[16,16,256]{2,1,0:T(8,128)(2,1)S(1)}, u32[]{:S(2)}, u32[]{:S(2)}) async-start(s16[16,16,256]{2,1,0:T(8,128)(2,1)} %get-tuple-element.9), calls=%async_computation | async-start | bytes 262144 | tf_op jit(solution)/shard_map/all_to_all | solution.py:357
  17.6 8.0 %collective-permute-start = (bf16[224,128]{1,0:T(8,128)(2,1)S(1)}, bf16[224,128]{1,0:T(8,128)(2,1)S(1)}, u32[]{:S(2)}, u32[]{:S(2)}) collective-permute-start(bf16[224,128]{1,0:T(8,128)(2,1)S(1)} %copy-done), channel_id=1, source_target_pairs={{0,16},{16,0},{1,17},{17,1},{2,18},{18,2},{3,19},{19,3},{4,20},{20... | collective-permute-start | bytes 172040 | tf_op jit(solution)/shard_map/ppermute | solution.py:372
  25.6 4.0 %all-to-all-done.val_ref = s16[16,16,256]{2,1,0:T(8,128)(2,1)S(1)} async-done(((s16[16,16,256]{2,1,0:T(8,128)(2,1)}), s16[16,16,256]{2,1,0:T(8,128)(2,1)S(1)}, u32[]{:S(2)}, u32[]{:S(2)}) %all-to-all-start) | async-done | bytes 131104 | tf_op jit(solution)/shard_map/all_to_all | solution.py:357
  29.7 0.0 copy-done.9
  29.7 0.0 copy-done.10
  29.7 7.3 %shard_map.168 = s16[16,16,256]{2,1,0:T(8,128)(2,1)} custom-call(s16[16,16,256]{2,1,0:T(8,128)(2,1)S(1)} %all-to-all-done.val_ref, s32[2,3584]{1,0:T(2,128)S(1)} %copy-done.14, s32[28,128]{1,0:T(8,128)S(1)} %bitcast.11, f32[8,128,128]{2,1,0:T(8,128)S(1)} %copy-done.1, bf16[256,256]{1,0:T(8,128)(2,1)S(1)} %copy-done.11, bf16[256,256]{1,0:T(8,128)(2,1)S(1)} %copy-done.10, ...), custom_call_target="tpu_custom_call" | custom-call | flops 1 | bytes 1 | tf_op jit(solution)/shard_map/pallas_call | solution.py:359
  37.0 0.0 collective-permute-done
  37.0 7.7 %all-to-all-start.1 = ((s16[16,16,256]{2,1,0:T(8,128)(2,1)}), s16[16,16,256]{2,1,0:T(8,128)(2,1)S(1)}, u32[]{:S(2)}, u32[]{:S(2)}) async-start(s16[16,16,256]{2,1,0:T(8,128)(2,1)} %shard_map.168), calls=%async_computation.1 | async-start | bytes 262144 | tf_op jit(solution)/shard_map/all_to_all | solution.py:379
  44.8 0.0 copy-start.4
  44.8 0.0 copy-start.5
  44.8 3.4 %collective-permute-start.1 = (bf16[2,224,128]{2,1,0:T(8,128)(2,1)S(1)}, bf16[2,224,128]{2,1,0:T(8,128)(2,1)S(1)}, u32[]{:S(2)}, u32[]{:S(2)}) collective-permute-start(bf16[2,224,128]{2,1,0:T(8,128)(2,1)S(1)} %pad_maximum_fusion.2), channel_id=1, source_target_pairs={{0,4},{4,0},{8,12},{12,8},{1,5},{5,1},{9,13},{13,9},{2,6},{6,2},{1... | collective-permute-start | bytes 344072 | tf_op jit(solution)/shard_map/ppermute | solution.py:375
  48.2 3.4 %collective-permute-done.1 = bf16[2,224,128]{2,1,0:T(8,128)(2,1)S(1)} collective-permute-done((bf16[2,224,128]{2,1,0:T(8,128)(2,1)S(1)}, bf16[2,224,128]{2,1,0:T(8,128)(2,1)S(1)}, u32[]{:S(2)}, u32[]{:S(2)}) %collective-permute-start.1) | collective-permute-done | bytes 114720 | tf_op jit(solution)/shard_map/ppermute | solution.py:375
  51.6 4.6 %collective-permute-start.2 = (bf16[4,224,128]{2,1,0:T(8,128)(2,1)S(1)}, bf16[4,224,128]{2,1,0:T(8,128)(2,1)S(1)}, u32[]{:S(2)}, u32[]{:S(2)}) collective-permute-start(bf16[4,224,128]{2,1,0:T(8,128)(2,1)S(1)} %pad_maximum_fusion.1), channel_id=1, source_target_pairs={{0,12},{4,8},{8,4},{12,0},{1,13},{5,9},{9,5},{13,1},{2,14},{6,10},... | collective-permute-start | bytes 688136 | tf_op jit(solution)/shard_map/ppermute | solution.py:377
  56.2 0.5 all-to-all-done.1.mix_ref
  56.8 1.3 %shard_map.169 = (f32[2,1,224,128]{3,2,1,0:T(8,128)}, bf16[4,2,224,128]{3,2,1,0:T(8,128)(2,1)}) custom-call(s16[16,16,256]{2,1,0:T(8,128)(2,1)S(1)} %all-to-all-done.1.mix_ref, f32[2,1,224,128]{3,2,1,0:T(8,128)S(1)} %copy-done.4, bf16[224,128]{1,0:T(8,128)(2,1)S(1)} %copy-done, f32[256,8]{1,0:T(8,128)S(1)} %copy-done.7, bf16[256,256]{1,0:T(8,128)(2,1)S(1)} %copy-done.6, ...), custom_call_target="tpu_custom_call" | custom-call | flops 100000000 | bytes 1000000 | tf_op jit(solution)/shard_map/pallas_call | solution.py:380
  58.1 4.0 %all-to-all-start.2 = ((bf16[4,2,224,128]{3,2,1,0:T(8,128)(2,1)}), bf16[4,2,224,128]{3,2,1,0:T(8,128)(2,1)S(1)}, u32[]{:S(2)}, u32[]{:S(2)}) async-start(bf16[4,2,224,128]{3,2,1,0:T(8,128)(2,1)} %get-tuple-element.15), calls=%async_computation.2 | async-start | bytes 917504 | tf_op jit(solution)/shard_map/all_to_all | solution.py:383
  62.1 0.0 collective-permute-done.2
  62.1 7.6 %all-to-all-done.2.pair_ref = bf16[4,2,224,128]{3,2,1,0:T(8,128)(2,1)S(1)} async-done(((bf16[4,2,224,128]{3,2,1,0:T(8,128)(2,1)}), bf16[4,2,224,128]{3,2,1,0:T(8,128)(2,1)S(1)}, u32[]{:S(2)}, u32[]{:S(2)}) %all-to-all-start.2) | async-done | bytes 458784 | tf_op jit(solution)/shard_map/all_to_all | solution.py:383
  69.7 1.5 %shard_map.170 = f32[8,128]{1,0:T(8,128)S(1)} custom-call(bf16[8,224,128]{2,1,0:T(8,128)(2,1)S(1)} %pad_maximum_fusion.left_ref, bf16[4,2,224,128]{3,2,1,0:T(8,128)(2,1)S(1)} %all-to-all-done.2.pair_ref), custom_call_target="tpu_custom_call" | custom-call | flops 100000000 | bytes 1000000 | tf_op jit(solution)/shard_map/pallas_call | solution.py:384
  71.2 22.5 %all_to_all.25 = f32[32,1,128]{2,1,0:T(1,128)S(1)} all-to-all(f32[32,1,128]{2,1,0:T(1,128)S(1)} %broadcast_in_dim.7), channel_id=1, replica_groups=mesh['zlo'=8,'core'=2,'zhi'=2,'y'=4,'x'=4] {'zlo','core','zhi'}, dimensions={0} | all-to-all | bytes 32768 | tf_op jit(solution)/shard_map/all_to_all | solution.py:391
  93.7 10.0 %all_to_all.26.columns_ref = f32[16,2,128]{2,1,0:T(2,128)S(1)} all-to-all(f32[16,2,128]{2,1,0:T(2,128)S(1)} %broadcast_in_dim.16), channel_id=1, replica_groups=mesh['zlo'=8,'core'=2,'zhi'=2,'y'=4,'x'=4] {'y','x'}, dimensions={0} | all-to-all | bytes 32768 | tf_op jit(solution)/shard_map/all_to_all | solution.py:394
  103.8 0.8 shard_map.171
  (26 shorter events, 0.2 us)
Async XLA Ops:
  0.6 29.0 %copy-start.1 = (f32[8,128,128]{2,1,0:T(8,128)S(1)}, f32[8,128,128]{2,1,0:T(8,128)}, u32[]{:S(2)}) copy-start(f32[8,128,128]{2,1,0:T(8,128)} %pot_ref.1) | copy-start | bytes 1572868
  0.6 29.0 %copy-start.2 = (bf16[2,256,256]{2,1,0:T(8,128)(2,1)S(1)}, bf16[2,256,256]{2,1,0:T(8,128)(2,1)}, u32[]{:S(2)}) copy-start(bf16[2,256,256]{2,1,0:T(8,128)(2,1)} %constant.35.clone.byl) | copy-start | bytes 786436
  0.7 29.0 %copy-start.3 = (bf16[2,256,256]{2,1,0:T(8,128)(2,1)S(1)}, bf16[2,256,256]{2,1,0:T(8,128)(2,1)}, u32[]{:S(2)}) copy-start(bf16[2,256,256]{2,1,0:T(8,128)(2,1)} %constant.34.clone.byh) | copy-start | bytes 786436
  0.7 29.0 %copy-start.9 = (bf16[256,144]{1,0:T(8,128)(2,1)S(1)}, bf16[256,144]{1,0:T(8,128)(2,1)}, u32[]{:S(2)}) copy-start(bf16[256,144]{1,0:T(8,128)(2,1)} %constant.30.clone.xh) | copy-start | bytes 221188
  0.7 29.0 %copy-start.10 = (bf16[256,256]{1,0:T(8,128)(2,1)S(1)}, bf16[256,256]{1,0:T(8,128)(2,1)}, u32[]{:S(2)}) copy-start(bf16[256,256]{1,0:T(8,128)(2,1)} %constant.29.clone.yl) | copy-start | bytes 393220
  0.7 29.0 %copy-start.11 = (bf16[256,256]{1,0:T(8,128)(2,1)S(1)}, bf16[256,256]{1,0:T(8,128)(2,1)}, u32[]{:S(2)}) copy-start(bf16[256,256]{1,0:T(8,128)(2,1)} %constant.28.clone.yh) | copy-start | bytes 393220
  0.7 29.0 %copy-start.13 = (bf16[144,256]{1,0:T(8,128)(2,1)S(1)}, bf16[144,256]{1,0:T(8,128)(2,1)}, u32[]{:S(2)}) copy-start(bf16[144,256]{1,0:T(8,128)(2,1)} %constant.32.clone.bxh) | copy-start | bytes 221188
  0.7 29.0 %copy-start.14 = (s32[2,3584]{1,0:T(2,128)S(1)}, s32[2,3584]{1,0:T(2,128)}, u32[]{:S(2)}) copy-start(s32[2,3584]{1,0:T(2,128)} %coords_ref.1) | copy-start | bytes 86020
  0.7 29.0 %copy-start.15 = (s32[3584]{0:T(1024)S(1)}, s32[3584]{0:T(1024)}, u32[]{:S(2)}) copy-start(s32[3584]{0:T(1024)} %param.19) | copy-start | bytes 43012
  3.4 14.2 %copy-start = (bf16[224,128]{1,0:T(8,128)(2,1)S(1)}, bf16[224,128]{1,0:T(8,128)(2,1)}, u32[]{:S(2)}) copy-start(bf16[224,128]{1,0:T(8,128)(2,1)} %get-tuple-element.10.left_ref) | copy-start | bytes 172036
  3.4 26.3 %copy-start.8 = (bf16[256,144]{1,0:T(8,128)(2,1)S(1)}, bf16[256,144]{1,0:T(8,128)(2,1)}, u32[]{:S(2)}) copy-start(bf16[256,144]{1,0:T(8,128)(2,1)} %constant.31.clone.xl) | copy-start | bytes 221188
  3.4 26.3 %copy-start.12 = (bf16[144,256]{1,0:T(8,128)(2,1)S(1)}, bf16[144,256]{1,0:T(8,128)(2,1)}, u32[]{:S(2)}) copy-start(bf16[144,256]{1,0:T(8,128)(2,1)} %constant.33.clone.bxl) | copy-start | bytes 221188
  3.4 26.2 %all-to-all-start = ((s16[16,16,256]{2,1,0:T(8,128)(2,1)}), s16[16,16,256]{2,1,0:T(8,128)(2,1)S(1)}, u32[]{:S(2)}, u32[]{:S(2)}) async-start(s16[16,16,256]{2,1,0:T(8,128)(2,1)} %get-tuple-element.9), calls=%async_computation | async-start | bytes 262144 | tf_op jit(solution)/shard_map/all_to_all | solution.py:357
  17.6 19.4 %collective-permute-start = (bf16[224,128]{1,0:T(8,128)(2,1)S(1)}, bf16[224,128]{1,0:T(8,128)(2,1)S(1)}, u32[]{:S(2)}, u32[]{:S(2)}) collective-permute-start(bf16[224,128]{1,0:T(8,128)(2,1)S(1)} %copy-done), channel_id=1, source_target_pairs={{0,16},{16,0},{1,17},{17,1},{2,18},{18,2},{3,19},{19,3},{4,20},{20... | collective-permute-start | bytes 172040 | tf_op jit(solution)/shard_map/ppermute | solution.py:372
  37.0 19.7 %all-to-all-start.1 = ((s16[16,16,256]{2,1,0:T(8,128)(2,1)}), s16[16,16,256]{2,1,0:T(8,128)(2,1)S(1)}, u32[]{:S(2)}, u32[]{:S(2)}) async-start(s16[16,16,256]{2,1,0:T(8,128)(2,1)} %shard_map.168), calls=%async_computation.1 | async-start | bytes 262144 | tf_op jit(solution)/shard_map/all_to_all | solution.py:379
  44.7 12.0 %copy-start.6 = (bf16[256,256]{1,0:T(8,128)(2,1)S(1)}, bf16[256,256]{1,0:T(8,128)(2,1)}, u32[]{:S(2)}) copy-start(bf16[256,256]{1,0:T(8,128)(2,1)} %constant.36.clone.high_ref) | copy-start | bytes 393220
  44.7 12.0 %copy-start.7 = (f32[256,8]{1,0:T(8,128)S(1)}, f32[256,8]{1,0:T(8,128)}, u32[]{:S(2)}) copy-start(f32[256,8]{1,0:T(8,128)} %get-tuple-element.12.cols_ref) | copy-start | bytes 24580
  44.8 12.0 %copy-start.4 = (f32[2,1,224,128]{3,2,1,0:T(8,128)S(1)}, f32[2,1,224,128]{3,2,1,0:T(8,128)}, u32[]{:S(2)}) copy-start(f32[2,1,224,128]{3,2,1,0:T(8,128)} %orb_ref.1) | copy-start | bytes 688132
  44.8 12.0 %copy-start.5 = (bf16[256,256]{1,0:T(8,128)(2,1)S(1)}, bf16[256,256]{1,0:T(8,128)(2,1)}, u32[]{:S(2)}) copy-start(bf16[256,256]{1,0:T(8,128)(2,1)} %constant.37.clone.low_ref) | copy-start | bytes 393220
  44.8 6.7 %collective-permute-start.1 = (bf16[2,224,128]{2,1,0:T(8,128)(2,1)S(1)}, bf16[2,224,128]{2,1,0:T(8,128)(2,1)S(1)}, u32[]{:S(2)}, u32[]{:S(2)}) collective-permute-start(bf16[2,224,128]{2,1,0:T(8,128)(2,1)S(1)} %pad_maximum_fusion.2), channel_id=1, source_target_pairs={{0,4},{4,0},{8,12},{12,8},{1,5},{5,1},{9,13},{13,9},{2,6},{6,2},{1... | collective-permute-start | bytes 344072 | tf_op jit(solution)/shard_map/ppermute | solution.py:375
  51.6 10.5 %collective-permute-start.2 = (bf16[4,224,128]{2,1,0:T(8,128)(2,1)S(1)}, bf16[4,224,128]{2,1,0:T(8,128)(2,1)S(1)}, u32[]{:S(2)}, u32[]{:S(2)}) collective-permute-start(bf16[4,224,128]{2,1,0:T(8,128)(2,1)S(1)} %pad_maximum_fusion.1), channel_id=1, source_target_pairs={{0,12},{4,8},{8,4},{12,0},{1,13},{5,9},{9,5},{13,1},{2,14},{6,10},... | collective-permute-start | bytes 688136 | tf_op jit(solution)/shard_map/ppermute | solution.py:377
  58.1 11.6 %all-to-all-start.2 = ((bf16[4,2,224,128]{3,2,1,0:T(8,128)(2,1)}), bf16[4,2,224,128]{3,2,1,0:T(8,128)(2,1)S(1)}, u32[]{:S(2)}, u32[]{:S(2)}) async-start(bf16[4,2,224,128]{3,2,1,0:T(8,128)(2,1)} %get-tuple-element.15), calls=%async_computation.2 | async-start | bytes 917504 | tf_op jit(solution)/shard_map/all_to_all | solution.py:383
